TPU v7x, 256 devices: a whole 4x4x8 slice. The times are simulated.
256 devices in a mesh: rows: 64 (over x, z, core), group: 4 (over y).
Axes of the slice: x: 4, y: 4, z: 8, core: 2. Of those that a mesh axis runs over, the one named last changes fastest.
Arguments:
- scores: bfloat16 [262144, 1024], P(('rows', 'group'))
- worker_ids: int32 [262144], P(('rows', 'group')), may hold values from 0 to 65535, as said below
- firm_ids: int32 [262144], P(('rows', 'group')), may hold values from 0 to 32767, as said below
Outputs:
- meat: float32 [1024, 1024], P('rows', 'group')
Inputs may be any that keep to these rules, and one draw needn't show every extreme that they name: `worker_ids`: among the rows of one device, at most 8 have worker ids of one residue mod 256, and on every device some residue has exactly 8. `firm_ids`: every worker names at most two firms. Among the rows of one device, at most 8 have firm ids of one residue mod 256, and on every device some residue has exactly 8. For any residues a and b mod 256, at most 2 distinct worker-firm pairs have a worker of residue a and a firm of residue b, and some a and b have exactly 2.
All inputs are finite; a program needn't handle non-finite values.
Results may differ from a plain program's by a relative error of at most 0.0035.
Values may be sent and summed in bfloat16 or wider, within the bound.
No kernel may reach another device: no remote copies, remote signals or barrier semaphores. Data moves between devices by JAX's collectives and lax.ppermute only.
A program may use at most 64 MiB of HBM per device.

v0:
```python
import jax
import jax.numpy as jnp
from jax import lax
from jax.sharding import PartitionSpec as P

CW_DEV = 256
CF_DEV = 128


def cluster_table(slot_ids, number):
    return jnp.arange(number, dtype=jnp.int32)[:, None] == slot_ids[None, :]


def collect(slot_ids, vectors, number):
    one_hot = cluster_table(slot_ids, number).astype(jnp.bfloat16)
    return jnp.dot(one_hot, vectors, preferred_element_type=jnp.float32)


def positions(homes, classes, capacity):
    matches = (homes[:, None] == jnp.arange(classes, dtype=jnp.int32)[None, :]).astype(jnp.int32)
    earlier = jnp.sum((jnp.cumsum(matches, axis=0) - matches) * matches, axis=1)
    return homes * capacity + earlier


def packed(target, values, filler, layout):
    slots = layout[0] * layout[1] * layout[2]
    buffer = jnp.full((slots,) + values.shape[1:], filler, values.dtype)
    return buffer.at[target].set(values, mode="drop").reshape(layout + values.shape[1:])


def pair_slots(flat_workers, flat_firms, worker_count):
    table = cluster_table(flat_workers, worker_count)
    first = jnp.min(jnp.where(table, flat_firms[None, :], 2**30), axis=1)
    row_first = jnp.max(jnp.where(table, first[:, None], -1), axis=0)
    ordinal = (flat_firms != row_first).astype(jnp.int32)
    return jnp.where(flat_workers >= 0, 2 * flat_workers + ordinal, -1)


def local(scores, worker_ids, firm_ids):
    row_count = lax.axis_size("rows")
    group_count = lax.axis_size("group")
    classes = row_count * group_count
    local_rows = scores.shape[0]
    feature_width = scores.shape[1]
    capacity = 2 * local_rows // classes
    layout = (row_count, group_count, capacity)
    worker_home = worker_ids % classes
    firm_home = firm_ids % classes
    worker_slot = worker_ids // classes
    firm_slot = firm_ids // classes
    worker_target = positions(worker_home, classes, capacity)
    worker_rows = packed(worker_target, scores, 0, layout)
    worker_locals = packed(worker_target, worker_slot, -1, layout)
    worker_firms = packed(worker_target, firm_ids, -1, layout)
    pair_total = 2 * CW_DEV
    firm_target = positions(firm_home, classes, capacity)
    firm_rows = packed(firm_target, scores, 0, layout)
    firm_slots = packed(firm_target, firm_slot, -1, layout)
    got_rows, got_workers, got_firms, got_firm_rows, got_slots = (
        lax.all_to_all(
            lax.all_to_all(worker_rows, "rows", split_axis=0, concat_axis=0, tiled=True),
            "group",
            split_axis=1,
            concat_axis=1,
            tiled=True,
        ),
        lax.all_to_all(
            lax.all_to_all(worker_locals, "rows", split_axis=0, concat_axis=0, tiled=True),
            "group",
            split_axis=1,
            concat_axis=1,
            tiled=True,
        ),
        lax.all_to_all(
            lax.all_to_all(worker_firms, "rows", split_axis=0, concat_axis=0, tiled=True),
            "group",
            split_axis=1,
            concat_axis=1,
            tiled=True,
        ),
        lax.all_to_all(
            lax.all_to_all(firm_rows, "rows", split_axis=0, concat_axis=0, tiled=True),
            "group",
            split_axis=1,
            concat_axis=1,
            tiled=True,
        ),
        lax.all_to_all(
            lax.all_to_all(firm_slots, "rows", split_axis=0, concat_axis=0, tiled=True),
            "group",
            split_axis=1,
            concat_axis=1,
            tiled=True,
        ),
    )
    flat_pairs = pair_slots(got_workers.reshape(-1), got_firms.reshape(-1), CW_DEV)
    pair_sums = collect(flat_pairs, got_rows.reshape(-1, feature_width), pair_total)
    firm_sums = collect(got_slots.reshape(-1), got_firm_rows.reshape(-1, feature_width), CF_DEV)
    split_pairs = pair_sums.reshape(CW_DEV, 2, feature_width)
    worker_sums = split_pairs[:, 0] + split_pairs[:, 1]
    left_side = jnp.concatenate([worker_sums, firm_sums, pair_sums], axis=0)
    right_side = jnp.concatenate([worker_sums, firm_sums, -pair_sums], axis=0)
    stacked = left_side.shape[0]
    block_rows = feature_width // row_count
    block_cols = feature_width // group_count
    term = jnp.einsum(
        "crk,cgl->rgkl",
        left_side.reshape(stacked, row_count, block_rows),
        right_side.reshape(stacked, group_count, block_cols),
        precision=lax.Precision.HIGHEST,
    ) * (1.0 / (classes * local_rows))
    totals = lax.psum(term, ("rows", "group"))
    picked = lax.dynamic_index_in_dim(totals, lax.axis_index("rows"), 0, keepdims=False)
    meat = lax.dynamic_index_in_dim(picked, lax.axis_index("group"), 0, keepdims=False)
    return meat


def solution(mesh):
    placed = (P(("rows", "group"), None), P(("rows", "group")), P(("rows", "group")))
    return jax.shard_map(
        local, mesh=mesh, in_specs=placed, out_specs=P("rows", "group"), check_vma=False
    )
```

profile of v0, /device:TPU:8, one launch (start us, length us, event | category | flops | bytes accessed | tf_op | source)
XLA Modules:
  0.0 720.2 jit_solution(12128999356887510797)
XLA Ops:
  6.5 0.8 add_select_fusion.4
  8.5 4.3 scatter_custom_fusion
  12.8 0.8 reshape.95
  13.7 11.9 %all-to-all-start = ((s32[64,4,8]{2,1,0:T(4,128)}), s32[64,4,8]{2,1,0:T(4,128)S(1)}, u32[]{:S(2)}, u32[]{:S(2)}) async-start(s32[64,4,8]{2,1,0:T(4,128)} %reshape.95), calls=%async_computation | async-start | bytes 262144 | tf_op jit(solution)/shard_map/all_to_all | solution.py:68
  26.8 4.3 scatter_custom_fusion.1
  31.1 0.8 reshape.97
  32.0 3.9 all-to-all-done
  35.9 6.4 all-to-all-start.2
  42.3 4.3 scatter_custom_fusion.3
  46.7 0.8 reshape.103
  47.5 5.1 all-to-all-done.2
  52.6 5.2 all-to-all-start.6
  57.9 0.7 reshape.167
  58.6 9.5 %all-to-all-done.6 = s32[64,4,8]{2,1,0:T(4,128)S(1)} async-done(((s32[64,4,8]{2,1,0:T(4,128)}), s32[64,4,8]{2,1,0:T(4,128)S(1)}, u32[]{:S(2)}, u32[]{:S(2)}) %all-to-all-start.6) | async-done | bytes 8224 | tf_op jit(solution)/shard_map/all_to_all | solution.py:89
  68.1 4.9 all-to-all-start.1
  73.1 0.7 reshape.169
  73.8 3.1 all-to-all-done.1
  76.9 4.7 all-to-all-start.3
  81.7 0.7 reshape.165
  82.4 3.1 all-to-all-done.3
  85.4 5.1 all-to-all-start.7
  90.6 8.6 %scatter_custom_fusion.2 = bf16[2048,1024]{1,0:T(8,128)(2,1)} fusion(s32[1024]{0:T(1024)S(1)} %get-tuple-element.10, bf16[1024,1024]{1,0:T(8,128)(2,1)} %param.3, bf16[]{:T(256)} %constant.98.clone.1), kind=kCustom, calls=%fused_computation.17 | custom fusion | bytes 4194816 | tf_op jit(solution)/shard_map/scatter | solution.py:28
  99.2 5.7 all-to-all-start.4
  104.9 8.6 %scatter_custom_fusion.4 = bf16[2048,1024]{1,0:T(8,128)(2,1)} fusion(s32[1024]{0:T(1024)S(1)} %get-tuple-element.14, bf16[1024,1024]{1,0:T(8,128)(2,1)} %param.3, bf16[]{:T(256)} %constant.98.clone.1), kind=kCustom, calls=%fused_computation.15 | custom fusion | bytes 4194816 | tf_op jit(solution)/shard_map/scatter | solution.py:28
  113.5 87.1 %all-to-all-done.4 = bf16[64,4,8,1024]{3,2,1,0:T(8,128)(2,1)} async-done(((bf16[64,4,8,1024]{3,2,1,0:T(8,128)(2,1)}), bf16[64,4,8,1024]{3,2,1,0:T(8,128)(2,1)}, u32[]{:S(2)}, u32[]{:S(2)}) %all-to-all-start.4) | async-done | bytes 4194336 | tf_op jit(solution)/shard_map/all_to_all | solution.py:61
  200.6 6.1 all-to-all-start.8
  206.7 4.8 copy.76
  211.5 90.9 %all-to-all-done.8 = bf16[64,4,8,1024]{3,2,1,0:T(8,128)(2,1)} async-done(((bf16[64,4,8,1024]{3,2,1,0:T(8,128)(2,1)}), bf16[64,4,8,1024]{3,2,1,0:T(8,128)(2,1)}, u32[]{:S(2)}, u32[]{:S(2)}) %all-to-all-start.8) | async-done | bytes 4194336 | tf_op jit(solution)/shard_map/all_to_all | solution.py:82
  302.4 5.1 all-to-all-start.5
  307.5 4.7 copy.84
  312.2 43.6 %all-to-all-done.5 = bf16[64,4,8,1024]{3,2,0,1:T(8,128)(2,1)} async-done(((bf16[64,4,8,1024]{3,2,0,1:T(8,128)(2,1)}), bf16[64,4,8,1024]{3,2,0,1:T(8,128)(2,1)}, u32[]{:S(2)}, u32[]{:S(2)}) %all-to-all-start.5) | async-done | bytes 4194336 | tf_op jit(solution)/shard_map/all_to_all | solution.py:60
  355.8 6.2 all-to-all-start.9
  362.5 0.7 reduce
  363.5 0.7 reduce.1
  364.6 0.7 reduce.2
  366.4 2.6 copy.77
  369.0 3.8 fusion.41
  372.8 2.2 reshape.101
  375.0 5.1 fusion.40
  380.0 29.4 %all-to-all-done.9 = bf16[64,4,8,1024]{3,2,0,1:T(8,128)(2,1)} async-done(((bf16[64,4,8,1024]{3,2,0,1:T(8,128)(2,1)}), bf16[64,4,8,1024]{3,2,0,1:T(8,128)(2,1)}, u32[]{:S(2)}, u32[]{:S(2)}) %all-to-all-start.9) | async-done | bytes 4194336 | tf_op jit(solution)/shard_map/all_to_all | solution.py:81
  409.5 2.6 copy.85
  412.1 0.7 fusion.24
  414.0 3.8 pad_maximum_fusion
  417.9 5.0 copy.86
  422.9 5.3 reshape.106
  428.2 19.1 %multiply_bitcast_fusion = f32[64,4,16,256]{3,0,2,1:T(8,128)} fusion(f32[896,64,16]{0,2,1:T(8,128)} %bitcast.54, f32[896,4,256,1]{2,1,0,3:T(4,128)} %bitcast.55), kind=kOutput, calls=%fused_computation.5 | convolution fusion | flops 11275337728 | bytes 11534336 | tf_op jit(solution)/shard_map/crk,cgl->rgkl/dot_general | solution.py:106
  447.3 264.3 %all-reduce.2.cloned.1.call-done = f32[64,4,16,256]{3,0,2,1:T(8,128)} async-done(((f32[64,4,16,256]{3,0,2,1:T(8,128)}), f32[64,4,16,256]{3,0,2,1:T(8,128)}) %all-reduce.2.cloned.1.call-update) | async-done | bytes 4194320 | tf_op jit(solution)/shard_map/psum | solution.py:112
  711.6 0.9 constant_dynamic-slice_fusion
  (48 shorter events, 6.6 us)
Async XLA Ops:
  6.5 1.9 copy-start.2
  6.5 19.1 %copy-start.3 = (s32[1024]{0:T(1024)S(1)}, s32[1024]{0:T(1024)}, u32[]{:S(2)}) copy-start(s32[1024]{0:T(1024)} %param.5) | copy-start | bytes 12292
  13.7 22.2 %all-to-all-start = ((s32[64,4,8]{2,1,0:T(4,128)}), s32[64,4,8]{2,1,0:T(4,128)S(1)}, u32[]{:S(2)}, u32[]{:S(2)}) async-start(s32[64,4,8]{2,1,0:T(4,128)} %reshape.95), calls=%async_computation | async-start | bytes 262144 | tf_op jit(solution)/shard_map/all_to_all | solution.py:68
  35.9 16.7 %all-to-all-start.2 = ((s32[64,4,8]{2,1,0:T(4,128)}), s32[64,4,8]{2,1,0:T(4,128)S(1)}, u32[]{:S(2)}, u32[]{:S(2)}) async-start(s32[64,4,8]{2,1,0:T(4,128)} %reshape.97), calls=%async_computation.2 | async-start | bytes 262144 | tf_op jit(solution)/shard_map/all_to_all | solution.py:75
  52.6 15.5 %all-to-all-start.6 = ((s32[64,4,8]{2,1,0:T(4,128)}), s32[64,4,8]{2,1,0:T(4,128)S(1)}, u32[]{:S(2)}, u32[]{:S(2)}) async-start(s32[64,4,8]{2,1,0:T(4,128)} %reshape.103), calls=%async_computation.6 | async-start | bytes 262144 | tf_op jit(solution)/shard_map/all_to_all | solution.py:89
  68.1 8.8 %all-to-all-start.1 = ((s32[4,1,512]{2,1,0:T(1,128)}), s32[4,1,512]{2,1,0:T(1,128)S(1)}, u32[]{:S(2)}, u32[]{:S(2)}) async-start(s32[4,1,512]{2,1,0:T(1,128)} %reshape.167), calls=%async_computation.1 | async-start | bytes 16384 | tf_op jit(solution)/shard_map/all_to_all | solution.py:67
  76.9 8.5 %all-to-all-start.3 = ((s32[4,1,512]{2,1,0:T(1,128)}), s32[4,1,512]{2,1,0:T(1,128)S(1)}, u32[]{:S(2)}, u32[]{:S(2)}) async-start(s32[4,1,512]{2,1,0:T(1,128)} %reshape.169), calls=%async_computation.3 | async-start | bytes 16384 | tf_op jit(solution)/shard_map/all_to_all | solution.py:74
  85.4 13.7 %all-to-all-start.7 = ((s32[4,1,512]{2,1,0:T(1,128)}), s32[4,1,512]{2,1,0:T(1,128)S(1)}, u32[]{:S(2)}, u32[]{:S(2)}) async-start(s32[4,1,512]{2,1,0:T(1,128)} %reshape.165), calls=%async_computation.7 | async-start | bytes 16384 | tf_op jit(solution)/shard_map/all_to_all | solution.py:88
  99.2 101.4 %all-to-all-start.4 = ((bf16[64,4,8,1024]{3,2,1,0:T(8,128)(2,1)}), bf16[64,4,8,1024]{3,2,1,0:T(8,128)(2,1)}, u32[]{:S(2)}, u32[]{:S(2)}) async-start(bf16[64,4,8,1024]{3,2,1,0:T(8,128)(2,1)} %bitcast.50), calls=%async_computation.4 | async-start | bytes 8388608 | tf_op jit(solution)/shard_map/all_to_all | solution.py:61
  200.6 101.8 %all-to-all-start.8 = ((bf16[64,4,8,1024]{3,2,1,0:T(8,128)(2,1)}), bf16[64,4,8,1024]{3,2,1,0:T(8,128)(2,1)}, u32[]{:S(2)}, u32[]{:S(2)}) async-start(bf16[64,4,8,1024]{3,2,1,0:T(8,128)(2,1)} %bitcast.51), calls=%async_computation.8 | async-start | bytes 8388608 | tf_op jit(solution)/shard_map/all_to_all | solution.py:82
  302.4 53.4 %all-to-all-start.5 = ((bf16[64,4,8,1024]{3,2,0,1:T(8,128)(2,1)}), bf16[64,4,8,1024]{3,2,0,1:T(8,128)(2,1)}, u32[]{:S(2)}, u32[]{:S(2)}) async-start(bf16[64,4,8,1024]{3,2,0,1:T(8,128)(2,1)} %copy.76), calls=%async_computation.5 | async-start | bytes 8388608 | tf_op jit(solution)/shard_map/all_to_all | solution.py:60
  355.8 53.7 %all-to-all-start.9 = ((bf16[64,4,8,1024]{3,2,0,1:T(8,128)(2,1)}), bf16[64,4,8,1024]{3,2,0,1:T(8,128)(2,1)}, u32[]{:S(2)}, u32[]{:S(2)}) async-start(bf16[64,4,8,1024]{3,2,0,1:T(8,128)(2,1)} %copy.84), calls=%async_computation.9 | async-start | bytes 8388608 | tf_op jit(solution)/shard_map/all_to_all | solution.py:81
  362.0 349.6 %all-reduce.2.cloned.1.call-start = ((), (), s32[]{:S(2)}) async-start(), calls=%async_computation.10 | async-start | bytes 8388608 | tf_op jit(solution)/shard_map/psum | solution.py:112
  412.1 1.2 copy-start
  412.1 1.9 copy-start.1
Sparse Core Ops, SparseCore 0:
  447.4 264.1 all-reduce.1
where the time goes:
time: 728 us; the launch traced here: 720 us
  waiting for transfers between devices  540 us (74%)
  local copies, waits for them, and re-layouts  72 us (10%)
  starting transfers between devices  61.4 us (8%)
  matrix products  23.6 us (3%)
  between operations  13.9 us (2%)
  other arithmetic  9.27 us (1%)
    psum x1, waiting for transfers between devices, local(): totals = lax.psum(term, ('rows', 'group'))  264 us
    all_to_all x1, waiting for transfers between devices, local(): lax.all_to_all(firm_rows, 'rows', split_axis=0, concat_axis=0, tiled=True)  90.9 us
    all_to_all x1, waiting for transfers between devices, local(): lax.all_to_all(worker_rows, 'rows', split_axis=0, concat_axis=0, tiled=True)  87.1 us
    all_to_all x1, waiting for transfers between devices, local(): lax.all_to_all(lax.all_to_all(worker_rows, 'rows', split_axis=0, concat_a...  43.6 us
    scatter x5, local copies, waits for them, and re-layouts, packed(): buffer.at[target].set(values, mode='drop')  30.1 us
    all_to_all x1, waiting for transfers between devices, local(): lax.all_to_all(lax.all_to_all(firm_rows, 'rows', split_axis=0, concat_axi...  29.4 us
    dot_general x1, matrix products, local(): jnp.einsum('crk,cgl->rgkl', left_side.reshape(stacked, row_count, block_r...  19.1 us
  transfers between devices with their start and end apart: 11, of which 10 were waited for; matrix products, arithmetic and copies ran while one was open for 8% of the time, Pallas kernels for 0%

commit v1 on v0

v1 whole, which is shorter than its diff:
```python
import jax
import jax.numpy as jnp
from jax import lax
from jax.sharding import PartitionSpec as P

LANES = 128


def equal_before(keys):
    index = jnp.arange(keys.shape[0], dtype=jnp.int32)
    same = (keys[:, None] == keys[None, :]) & (index[:, None] < index[None, :])
    return jnp.sum(same.astype(jnp.int32), axis=0)


def one_hot(targets, number):
    rows = lax.broadcasted_iota(jnp.int32, (number, targets.shape[0]), 0)
    return (rows == targets[None, :]).astype(jnp.bfloat16)


def placed_values(targets, values, number):
    rows = lax.broadcasted_iota(jnp.int32, (number, targets.shape[0]), 0)
    return jnp.max(jnp.where(rows == targets[None, :], values[None, :], -1), axis=1)


def dot(a, b):
    return jnp.dot(a, b, preferred_element_type=jnp.float32)


def solution(mesh):
    row_count, group_count = mesh.shape["rows"], mesh.shape["group"]
    classes = row_count * group_count
    everyone = ("rows", "group")
    workers_here = 65536 // classes
    firms_here = 32768 // classes
    firms = 32768

    def local(scores, worker_ids, firm_ids):
        local_rows, width = scores.shape
        capacity = 2 * local_rows // classes

        home = worker_ids % classes
        target = home * capacity + equal_before(home)
        code = (worker_ids // classes) * firms + firm_ids
        slot_codes = placed_values(target, code, classes * capacity)
        codes = lax.all_to_all(
            slot_codes.reshape(classes, capacity), everyone, 0, 0, tiled=True
        ).reshape(-1)
        packed = dot(one_hot(target, classes * capacity), scores).astype(jnp.bfloat16)
        got = lax.all_to_all(packed, everyone, 0, 0, tiled=True)

        used = codes >= 0
        worker = jnp.where(used, codes // firms, -1)
        firm = jnp.where(used, codes % firms, -1)
        table = lax.broadcasted_iota(jnp.int32, (workers_here, codes.shape[0]), 0) == worker[None, :]
        first = jnp.min(jnp.where(table, firm[None, :], 2**30), axis=1)
        row_first = jnp.max(jnp.where(table, first[:, None], -1), axis=0)
        pair = jnp.where(used, worker + workers_here * (firm != row_first).astype(jnp.int32), -1)
        pair_firm = placed_values(pair, firm, 2 * workers_here)
        firm_home = jnp.where(pair_firm >= 0, pair_firm % classes, -1)
        pair_slot = jnp.where(pair_firm >= 0, 2 * firm_home + equal_before(firm_home), -1)
        pair_rows = lax.broadcasted_iota(jnp.int32, (2 * workers_here, codes.shape[0]), 0)
        row_slot = jnp.max(jnp.where(pair_rows == pair[None, :], pair_slot[:, None], -1), axis=0)

        sent = dot(one_hot(row_slot, 2 * classes), got).astype(jnp.bfloat16)
        sent_firm = placed_values(pair_slot, pair_firm // classes, 2 * classes)
        tail = jnp.broadcast_to(sent_firm.astype(jnp.bfloat16)[:, None], (2 * classes, LANES))
        came = lax.all_to_all(
            jnp.concatenate([sent, tail], axis=1), everyone, 0, 0, tiled=True
        )
        pairs = dot(one_hot(pair, 2 * workers_here), got).astype(jnp.bfloat16)
        firm_local = came[:, width].astype(jnp.int32)
        firm_sums = dot(one_hot(firm_local, firms_here), came[:, :width]).astype(jnp.bfloat16)

        left = jnp.concatenate([pairs, firm_sums], axis=0)
        right = jnp.concatenate([pairs[workers_here:], pairs[:workers_here], firm_sums], axis=0)
        term = lax.dot_general(
            left, right, (((0,), (0,)), ((), ())), preferred_element_type=jnp.float32
        ).astype(jnp.bfloat16)
        block_rows, block_cols = width // row_count, width // group_count
        blocks = term.reshape(row_count, block_rows, group_count, block_cols)
        blocks = blocks.transpose(0, 2, 1, 3).reshape(classes, block_rows, block_cols)
        terms = lax.all_to_all(blocks, everyone, 0, 0, tiled=True)
        total = jnp.sum(terms.astype(jnp.float32), axis=0)
        return total * (1.0 / (classes * local_rows))

    placed = (P(everyone, None), P(everyone), P(everyone))
    return jax.shard_map(
        local, mesh=mesh, in_specs=placed, out_specs=P("rows", "group"), check_vma=False
    )
```

time: 728 us -> 264 us (0.36)
  waiting for transfers between devices: 540 us -> 129 us
  blocking collectives: 0 us -> 60.5 us
  local copies, waits for them, and re-layouts: 72 us -> 12.7 us
  starting transfers between devices: 61.4 us -> 29.6 us
  between operations: 13.9 us -> 0.15 us
    psum x1 -> x0, waiting for transfers between devices: 264 us -> none  [local(): totals = lax.psum(term, ('rows', 'group'))]
    all_to_all x10 -> x3, waiting for transfers between devices: 276 us -> 129 us  [the longest x1 94.2 us: local(): got = lax.all_to_all(packed, everyone, 0, 0, tiled=True)]
    all_to_all x0 -> x1, blocking collectives: none -> 60.5 us  [local(): terms = lax.all_to_all(blocks, everyone, 0, 0, tiled=True)]
    all_to_all x10 -> x3, starting transfers between devices: 61.4 us -> 29.6 us  [the longest x1 14.6 us: local(): lax.all_to_all(slot_codes.reshape(classes, capacity), everyone, 0, 0, til...]
    scatter x5 -> x0, local copies, waits for them, and re-layouts: 30.1 us -> none  [packed(): buffer.at[target].set(values, mode='drop')]
    all_to_all x11 -> x4, local copies, waits for them, and re-layouts: 15.8 us -> 3.81 us  [the longest x2 2.56 us: local(): lax.all_to_all(jnp.concatenate([sent, tail], axis=1), everyone, 0, 0, til...]
    dot_general x3 -> x5, matrix products: 23.6 us -> 21.3 us  [the longest x4 16.6 us: dot(): return jnp.dot(a, b, preferred_element_type=jnp.float32)]
  transfers between devices with their start and end apart: 11 -> 3, of which waited for: 10 -> 3; matrix products, arithmetic and copies ran while one was open for 8% -> 6% of each run, Pallas kernels for 0% -> 0%
where the time goes in v1:
time: 264 us; the launch traced here: 262 us
  waiting for transfers between devices  129 us (49%)
  blocking collectives  60.5 us (23%)
  starting transfers between devices  29.6 us (11%)
  matrix products  21.3 us (8%)
  local copies, waits for them, and re-layouts  12.7 us (5%)
  other arithmetic  8.73 us (3%)
    all_to_all x1, waiting for transfers between devices, local(): got = lax.all_to_all(packed, everyone, 0, 0, tiled=True)  94.2 us
    all_to_all x1, blocking collectives, local(): terms = lax.all_to_all(blocks, everyone, 0, 0, tiled=True)  60.5 us
    all_to_all x1, waiting for transfers between devices, local(): lax.all_to_all(jnp.concatenate([sent, tail], axis=1), everyone, 0, 0, til...  28.2 us
    dot_general x4, matrix products, dot(): return jnp.dot(a, b, preferred_element_type=jnp.float32)  16.6 us
    all_to_all x1, starting transfers between devices, local(): lax.all_to_all(slot_codes.reshape(classes, capacity), everyone, 0, 0, til...  14.6 us
    all_to_all x1, starting transfers between devices, local(): got = lax.all_to_all(packed, everyone, 0, 0, tiled=True)  8.45 us
    reshape x2, local copies, waits for them, and re-layouts, local(): blocks = term.reshape(row_count, block_rows, group_count, block_cols)  6.58 us
    all_to_all x1, starting transfers between devices, local(): lax.all_to_all(jnp.concatenate([sent, tail], axis=1), everyone, 0, 0, til...  6.49 us
  transfers between devices with their start and end apart: 3, of which 3 were waited for; matrix products, arithmetic and copies ran while one was open for 6% of the time, Pallas kernels for 0%

profile of v1, /device:TPU:8, one launch (start us, length us, event | category | flops | bytes accessed | tf_op | source)
XLA Modules:
  0.0 261.6 jit_solution(5041203716058756893)
XLA Ops:
  0.0 0.0 copy-start
  0.0 0.8 add_select_fusion.4
  0.8 0.4 convert_reduce_fusion.1
  1.3 0.7 multiply_add_fusion
  2.0 1.2 select_reduce_fusion
  3.2 0.7 all_to_all.25
  3.9 14.6 %all-to-all-start = ((s32[256,1,8]{2,1,0:T(1,128)}), s32[256,1,8]{2,1,0:T(1,128)S(1)}, u32[]{:S(2)}, u32[]{:S(2)}) async-start(s32[256,1,8]{2,1,0:T(1,128)} %bitcast), calls=%async_computation | async-start | bytes 262144 | tf_op jit(solution)/shard_map/all_to_all | solution.py:45
  18.5 0.0 copy-done
  18.5 6.0 %convert_bitcast_fusion = bf16[256,8,1024]{2,1,0:T(8,128)(2,1)} fusion(bf16[1024,1024]{1,0:T(8,128)(2,1)S(1)} %copy-done, s32[1024]{0:T(1024)S(1)} %get-tuple-element.9), kind=kOutput, calls=%fused_computation.11 | convolution fusion | flops 4299161600 | bytes 6295552 | tf_op jit(solution)/shard_map/dot_general | solution.py:26
  24.6 6.3 %all-to-all-done = s32[256,1,8]{2,1,0:T(1,128)S(1)} async-done(((s32[256,1,8]{2,1,0:T(1,128)}), s32[256,1,8]{2,1,0:T(1,128)S(1)}, u32[]{:S(2)}, u32[]{:S(2)}) %all-to-all-start) | async-done | bytes 8224 | tf_op jit(solution)/shard_map/all_to_all | solution.py:45
  30.9 8.5 %all-to-all-start.1 = ((bf16[256,8,1024]{2,1,0:T(8,128)(2,1)}), bf16[256,8,1024]{2,1,0:T(8,128)(2,1)}, u32[]{:S(2)}, u32[]{:S(2)}) async-start(bf16[256,8,1024]{2,1,0:T(8,128)(2,1)} %convert_bitcast_fusion), calls=%async_computation.1 | async-start | bytes 8388608 | tf_op jit(solution)/shard_map/all_to_all | solution.py:49
  39.3 0.5 broadcast.319
  39.8 1.0 reduce.5
  40.8 0.1 reshape.177
  40.9 0.4 select_reduce_fusion.4
  41.3 0.4 select_reduce_fusion.3
  41.7 0.6 select_reduce_fusion.2
  42.4 0.2 convert_reduce_fusion.2
  42.6 0.2 select_reduce_fusion.5
  42.8 0.7 select_reduce_fusion.1
  43.5 94.2 %all-to-all-done.1 = bf16[256,8,1024]{2,1,0:T(8,128)(2,1)} async-done(((bf16[256,8,1024]{2,1,0:T(8,128)(2,1)}), bf16[256,8,1024]{2,1,0:T(8,128)(2,1)}, u32[]{:S(2)}, u32[]{:S(2)}) %all-to-all-start.1) | async-done | bytes 4194336 | tf_op jit(solution)/shard_map/all_to_all | solution.py:49
  137.7 4.5 %fusion.12 = bf16[512,1024]{1,0:T(8,128)(2,1)S(1)} fusion(bf16[256,8,1024]{2,1,0:T(8,128)(2,1)} %all-to-all-done.1, s32[2048]{0:T(1024)S(1)} %select_reduce_fusion.1), kind=kOutput, calls=%fused_computation.26 | convolution fusion | flops 2149056512 | bytes 5251072 | tf_op jit(solution)/shard_map/dot_general | solution.py:26
  142.2 0.1 broadcast_in_dim.120
  142.3 0.1 pad_maximum_fusion.4
  142.4 1.3 all_to_all.30
  143.7 6.5 %all-to-all-start.2 = ((bf16[256,2,1152]{2,1,0:T(2,128)(2,1)}), bf16[256,2,1152]{2,1,0:T(2,128)(2,1)S(1)}, u32[]{:S(2)}, u32[]{:S(2)}) async-start(bf16[256,2,1152]{2,1,0:T(2,128)(2,1)} %all_to_all.30), calls=%async_computation.2 | async-start | bytes 2359296 | tf_op jit(solution)/shard_map/all_to_all | solution.py:67
  150.2 4.5 %fusion.9 = bf16[512,1024]{1,0:T(8,128)(2,1)S(1)} fusion(bf16[256,8,1024]{2,1,0:T(8,128)(2,1)} %all-to-all-done.1, s32[2048]{0:T(1024)S(1)} %add_select_fusion.2), kind=kOutput, calls=%fused_computation.25 | convolution fusion | flops 2149056512 | bytes 5251072 | tf_op jit(solution)/shard_map/dot_general | solution.py:26
  154.8 0.0 copy-start.1
  154.8 1.0 copy-done.1
  155.8 1.0 fusion.33
  156.8 28.2 %all-to-all-done.2 = bf16[256,2,1152]{2,1,0:T(2,128)(2,1)S(1)} async-done(((bf16[256,2,1152]{2,1,0:T(2,128)(2,1)}), bf16[256,2,1152]{2,1,0:T(2,128)(2,1)S(1)}, u32[]{:S(2)}, u32[]{:S(2)}) %all-to-all-start.2) | async-done | bytes 1179680 | tf_op jit(solution)/shard_map/all_to_all | solution.py:67
  185.0 1.3 all_to_all.32
  186.2 1.1 convert_reduce_fusion.3
  187.3 1.5 convolution_convert_fusion.1
  188.8 4.7 %convolution_convert_fusion = bf16[1024,1024]{1,0:T(8,128)(2,1)} fusion(bf16[128,1024]{1,0:T(8,128)(2,1)S(1)} %convolution_convert_fusion.1, bf16[512,1024]{1,0:T(8,128)(2,1)} %copy-done.1, bf16[256,1024]{1,0:T(8,128)(2,1)} %get-tuple-element.6, bf16[256,1024]{1,0:T(8,128)(2,1)} %get-tuple-element.5), kind=kOutput, calls=%fused_computation.22 | convolution fusion | flops 1349779456 | bytes 4456448 | tf_op jit(solution)/shard_map/dot_general | solution.py:76
  193.5 4.5 %reshape.178 = bf16[64,16,4,256]{3,2,1,0:T(4,128)(2,1)} reshape(bf16[1024,1024]{1,0:T(8,128)(2,1)} %convolution_convert_fusion) | data formatting | bytes 4194304 | tf_op jit(solution)/shard_map/reshape | solution.py:80
  198.1 2.1 copy.10
  200.1 60.5 %all_to_all.38 = bf16[256,16,256]{2,1,0:T(8,128)(2,1)S(1)} all-to-all(bf16[256,16,256]{2,1,0:T(8,128)(2,1)S(1)} %bitcast.16), channel_id=1, replica_groups=mesh['rows'=64,'group'=4] {'rows','group'}, dimensions={0} | all-to-all | bytes 4194304 | tf_op jit(solution)/shard_map/all_to_all | solution.py:82
  260.7 0.3 convert_reduce_fusion
  261.0 0.6 broadcast_multiply_fusion
  (5 shorter events, 0.1 us)
Async XLA Ops:
  0.0 18.5 %copy-start = (bf16[1024,1024]{1,0:T(8,128)(2,1)S(1)}, bf16[1024,1024]{1,0:T(8,128)(2,1)}, u32[]{:S(2)}) copy-start(bf16[1024,1024]{1,0:T(8,128)(2,1)} %param.3) | copy-start | bytes 6291460
  3.9 26.9 %all-to-all-start = ((s32[256,1,8]{2,1,0:T(1,128)}), s32[256,1,8]{2,1,0:T(1,128)S(1)}, u32[]{:S(2)}, u32[]{:S(2)}) async-start(s32[256,1,8]{2,1,0:T(1,128)} %bitcast), calls=%async_computation | async-start | bytes 262144 | tf_op jit(solution)/shard_map/all_to_all | solution.py:45
  30.9 106.8 %all-to-all-start.1 = ((bf16[256,8,1024]{2,1,0:T(8,128)(2,1)}), bf16[256,8,1024]{2,1,0:T(8,128)(2,1)}, u32[]{:S(2)}, u32[]{:S(2)}) async-start(bf16[256,8,1024]{2,1,0:T(8,128)(2,1)} %convert_bitcast_fusion), calls=%async_computation.1 | async-start | bytes 8388608 | tf_op jit(solution)/shard_map/all_to_all | solution.py:49
  143.7 41.2 %all-to-all-start.2 = ((bf16[256,2,1152]{2,1,0:T(2,128)(2,1)}), bf16[256,2,1152]{2,1,0:T(2,128)(2,1)S(1)}, u32[]{:S(2)}, u32[]{:S(2)}) async-start(bf16[256,2,1152]{2,1,0:T(2,128)(2,1)} %all_to_all.30), calls=%async_computation.2 | async-start | bytes 2359296 | tf_op jit(solution)/shard_map/all_to_all | solution.py:67
  154.8 1.0 copy-start.1

commit v2 on v1

v2 whole, which is shorter than its diff:
```python
import jax
import jax.numpy as jnp
from jax import lax
from jax.sharding import Mesh, PartitionSpec as P

AXES = ("x", "z", "core", "group")
EVERYONE = AXES
LANES = 128
FIRMS = 32768
WORKERS = 65536


def equal_before(keys):
    index = jnp.arange(keys.shape[0], dtype=jnp.int32)
    same = (keys[:, None] == keys[None, :]) & (index[:, None] < index[None, :])
    return jnp.sum(same.astype(jnp.int32), axis=0)


def one_hot(targets, number):
    rows = lax.broadcasted_iota(jnp.int32, (number, targets.shape[0]), 0)
    return (rows == targets[None, :]).astype(jnp.bfloat16)


def placed_values(targets, values, number):
    rows = lax.broadcasted_iota(jnp.int32, (number, targets.shape[0]), 0)
    return jnp.max(jnp.where(rows == targets[None, :], values[None, :], -1), axis=1)


def dot(a, b):
    return jnp.dot(a, b, preferred_element_type=jnp.float32)


def gram(a, b):
    return lax.dot_general(a, b, (((0,), (0,)), ((), ())), preferred_element_type=jnp.float32)


def swapped(value, axis, bit):
    size = lax.axis_size(axis)
    return lax.ppermute(value, axis, [(i, i ^ bit) for i in range(size)])


def exchange(blocks):
    classes, k = blocks.shape
    held = blocks.reshape(-1)
    before = 1
    for axis in AXES:
        bit = lax.axis_size(axis) // 2
        while bit:
            view = held.reshape(before, 2, -1)
            high = (lax.axis_index(axis) & bit) > 0
            keep = jnp.where(high, view[:, 1], view[:, 0])
            send = jnp.where(high, view[:, 0], view[:, 1])
            came = swapped(send, axis, bit)
            low_part = jnp.where(high, came, keep)
            high_part = jnp.where(high, keep, came)
            held = jnp.stack([low_part, high_part], axis=1).reshape(-1)
            before *= 2
            bit //= 2
    return held.reshape(classes, k)


def solution(mesh):
    row_count, group_count = mesh.shape["rows"], mesh.shape["group"]
    classes = row_count * group_count
    planes = row_count // 2
    fine = Mesh(mesh.devices.reshape(4, row_count // 8, 2, group_count), AXES)
    workers_here = WORKERS // classes
    firms_here = FIRMS // classes

    def local(scores, worker_ids, firm_ids):
        local_rows, width = scores.shape
        capacity = 2 * local_rows // classes
        core = lax.axis_index("core")

        home = worker_ids % classes
        target = home * capacity + equal_before(home)
        packed = dot(one_hot(target, classes * capacity), scores).astype(jnp.bfloat16)
        got = lax.all_to_all(packed, EVERYONE, 0, 0, tiled=True)
        code = (worker_ids // classes) * FIRMS + firm_ids
        slot_codes = placed_values(target, code, classes * capacity)
        codes = exchange(slot_codes.reshape(classes, capacity)).reshape(-1)

        used = codes >= 0
        worker = jnp.where(used, codes // FIRMS, -1)
        firm = jnp.where(used, codes % FIRMS, -1)
        table = lax.broadcasted_iota(jnp.int32, (workers_here, codes.shape[0]), 0) == worker[None, :]
        first = jnp.min(jnp.where(table, firm[None, :], 2**30), axis=1)
        row_first = jnp.max(jnp.where(table, first[:, None], -1), axis=0)
        pair = jnp.where(used, worker + workers_here * (firm != row_first).astype(jnp.int32), -1)
        pair_firm = placed_values(pair, firm, 2 * workers_here)
        firm_home = jnp.where(pair_firm >= 0, pair_firm % classes, -1)
        pair_slot = jnp.where(pair_firm >= 0, 2 * firm_home + equal_before(firm_home), -1)
        pair_rows = lax.broadcasted_iota(jnp.int32, (2 * workers_here, codes.shape[0]), 0)
        row_slot = jnp.max(jnp.where(pair_rows == pair[None, :], pair_slot[:, None], -1), axis=0)
        sent_firm = placed_values(pair_slot, pair_firm // classes, 2 * classes)

        sent = dot(one_hot(row_slot, 2 * classes), got).astype(jnp.bfloat16)
        tail = jnp.broadcast_to(sent_firm.astype(jnp.bfloat16)[:, None], (2 * classes, LANES))
        came = lax.all_to_all(
            jnp.concatenate([sent, tail], axis=1), EVERYONE, 0, 0, tiled=True
        )

        pairs = dot(one_hot(pair, 2 * workers_here), got).astype(jnp.bfloat16)
        more = swapped(pairs, "core", 1)
        half = workers_here
        left = jnp.concatenate([pairs, more], axis=0)
        right = jnp.concatenate([pairs[half:], pairs[:half], more[half:], more[:half]], axis=0)
        block_rows, block_cols = width // row_count, width // group_count
        picked = jnp.arange(width // 2, dtype=jnp.int32)
        picked = (picked // block_rows * 2 + core) * block_rows + picked % block_rows
        pick = one_hot(picked, width)
        left = dot(left, pick).astype(jnp.bfloat16)
        worker_terms = [
            gram(left, right[:, g * block_cols : (g + 1) * block_cols]) for g in range(group_count)
        ]

        came, worker_terms = lax.optimization_barrier((came, worker_terms))
        firm_local = came[:, width].astype(jnp.int32)
        firm_sums = dot(one_hot(firm_local, firms_here), came[:, :width])
        high = lax.optimization_barrier(firm_sums.astype(jnp.bfloat16))
        low = (firm_sums - high.astype(jnp.float32)).astype(jnp.bfloat16)
        firm_pair = jnp.concatenate([high, low], axis=0)
        firm_pair = jnp.concatenate([firm_pair, swapped(firm_pair, "core", 1)], axis=0)
        firm_left = dot(firm_pair, pick).astype(jnp.bfloat16)
        n = firms_here
        firm_left = jnp.concatenate([firm_left, firm_left[:n], firm_left[2 * n : 3 * n]], axis=0)
        firm_right = jnp.concatenate(
            [firm_pair[:n], firm_pair[:n], firm_pair[2 * n : 3 * n], firm_pair[2 * n : 3 * n],
             firm_pair[n : 2 * n], firm_pair[3 * n :]],
            axis=0,
        )
        terms = jnp.stack(
            [
                (worker_terms[g] + gram(firm_left, firm_right[:, g * block_cols : (g + 1) * block_cols])).astype(
                    jnp.bfloat16
                )
                for g in range(group_count)
            ]
        )
        terms = lax.all_to_all(terms, "group", 0, 0, tiled=True)
        wide = [terms[g].astype(jnp.float32) for g in range(group_count)]
        terms = sum(wide[1:], wide[0])
        terms = lax.all_to_all(
            terms.reshape(planes, block_rows, block_cols), ("x", "z"), 0, 0, tiled=True
        )
        total = jnp.sum(terms, axis=0)
        return total * (1.0 / (classes * local_rows))

    placed = (P(EVERYONE, None), P(EVERYONE), P(EVERYONE))
    return jax.shard_map(
        local, mesh=fine, in_specs=placed, out_specs=P(("x", "z", "core"), "group"), check_vma=False
    )
```

time: 264 us -> 248 us (0.939)
  blocking collectives: 60.5 us -> 37.9 us
  starting transfers between devices: 29.6 us -> 41.6 us
  waiting for transfers between devices: 129 us -> 121 us
  matrix products: 21.3 us -> 28 us
  local copies, waits for them, and re-layouts: 12.7 us -> 8.15 us
    all_to_all x3 -> x2, waiting for transfers between devices: 129 us -> 23.9 us  [the longest x1 23.9 us: local(): lax.all_to_all(jnp.concatenate([sent, tail], axis=1), EVERYONE, 0, 0, til...]
    ppermute x0 -> x10, waiting for transfers between devices: none -> 97 us  [swapped(): return lax.ppermute(value, axis, [(i, i ^ bit) for i in range(size)])]
    all_to_all x1 -> x2, blocking collectives: 60.5 us -> 37.9 us  [the longest x1 19.9 us: local(): lax.all_to_all(terms.reshape(planes, block_rows, block_cols), ('x', 'z'),...]
    ppermute x0 -> x10, starting transfers between devices: none -> 17.8 us  [swapped(): return lax.ppermute(value, axis, [(i, i ^ bit) for i in range(size)])]
    reshape x3 -> x0, local copies, waits for them, and re-layouts: 6.69 us -> none  [the longest x2 6.58 us: local(): blocks = term.reshape(row_count, block_rows, group_count, block_cols)]
    all_to_all x3 -> x2, starting transfers between devices: 29.6 us -> 23.8 us  [the longest x1 15.6 us: local(): got = lax.all_to_all(packed, EVERYONE, 0, 0, tiled=True)]
    dot_general x4 -> x6, matrix products: 16.6 us -> 21.2 us  [dot(): return jnp.dot(a, b, preferred_element_type=jnp.float32)]
    dot_general x1 -> x8, matrix products: 4.71 us -> 6.83 us  [gram(): lax.dot_general(a, b, (((0,), (0,)), ((), ())), preferred_element_type=jn...]
  transfers between devices with their start and end apart: 3 -> 12, of which waited for: 3 -> 10; matrix products, arithmetic and copies ran while one was open for 6% -> 8% of each run, Pallas kernels for 0% -> 0%
where the time goes in v2:
time: 248 us; the launch traced here: 246 us
  waiting for transfers between devices  121 us (49%)
  starting transfers between devices  41.6 us (17%)
  blocking collectives  37.9 us (15%)
  matrix products  28 us (11%)
  other arithmetic  8.45 us (3%)
  local copies, waits for them, and re-layouts  8.15 us (3%)
    ppermute x10, waiting for transfers between devices, swapped(): return lax.ppermute(value, axis, [(i, i ^ bit) for i in range(size)])  97 us
    all_to_all x1, waiting for transfers between devices, local(): lax.all_to_all(jnp.concatenate([sent, tail], axis=1), EVERYONE, 0, 0, til...  23.9 us
    dot_general x6, matrix products, dot(): return jnp.dot(a, b, preferred_element_type=jnp.float32)  21.2 us
    all_to_all x1, blocking collectives, local(): lax.all_to_all(terms.reshape(planes, block_rows, block_cols), ('x', 'z'),...  19.9 us
    all_to_all x1, blocking collectives, local(): terms = lax.all_to_all(terms, 'group', 0, 0, tiled=True)  18 us
    ppermute x10, starting transfers between devices, swapped(): return lax.ppermute(value, axis, [(i, i ^ bit) for i in range(size)])  17.8 us
    all_to_all x1, starting transfers between devices, local(): got = lax.all_to_all(packed, EVERYONE, 0, 0, tiled=True)  15.6 us
    all_to_all x1, starting transfers between devices, local(): lax.all_to_all(jnp.concatenate([sent, tail], axis=1), EVERYONE, 0, 0, til...  8.22 us
  transfers between devices with their start and end apart: 12, of which 10 were waited for; matrix products, arithmetic and copies ran while one was open for 8% of the time, Pallas kernels for 0%

profile of v2, /device:TPU:8, one launch (start us, length us, event | category | flops | bytes accessed | tf_op | source)
XLA Modules:
  0.0 245.6 jit_solution(16469294184818240665)
XLA Ops:
  0.0 0.8 add_select_fusion.4
  1.3 0.7 multiply_add_fusion
  2.0 6.0 %convert_bitcast_fusion = bf16[256,8,1024]{2,1,0:T(8,128)(2,1)} fusion(bf16[1024,1024]{1,0:T(8,128)(2,1)S(1)} %copy-done, s32[1024]{0:T(1024)S(1)} %get-tuple-element.57), kind=kOutput, calls=%fused_computation.7 | convolution fusion | flops 4299161600 | bytes 6295552 | tf_op jit(solution)/shard_map/dot_general | solution.py:30
  8.0 15.6 %all-to-all-start = ((bf16[256,8,1024]{2,1,0:T(8,128)(2,1)}), bf16[256,8,1024]{2,1,0:T(8,128)(2,1)}, u32[]{:S(2)}, u32[]{:S(2)}) async-start(bf16[256,8,1024]{2,1,0:T(8,128)(2,1)} %convert_bitcast_fusion), calls=%async_computation | async-start | bytes 8388608 | tf_op jit(solution)/shard_map/all_to_all | solution.py:78
  23.7 1.2 select_reduce_fusion
  24.9 3.1 %collective-permute-start = (s32[1,1024]{1,0:T(1,128)S(1)}, s32[1,1024]{1,0:T(1,128)S(1)}, u32[]{:S(2)}, u32[]{:S(2)}) collective-permute-start(s32[1,1024]{1,0:T(1,128)S(1)} %fusion.61), channel_id=1, source_target_pairs={{0,128},{64,192},{128,0},{192,64},{1,129},{65,193},{129,1},{193,65... | collective-permute-start | bytes 12296 | tf_op jit(solution)/shard_map/ppermute | solution.py:39
  27.9 5.1 %collective-permute-done = s32[1,1024]{1,0:T(1,128)S(1)} collective-permute-done((s32[1,1024]{1,0:T(1,128)S(1)}, s32[1,1024]{1,0:T(1,128)S(1)}, u32[]{:S(2)}, u32[]{:S(2)}) %collective-permute-start) | collective-permute-done | bytes 4128 | tf_op jit(solution)/shard_map/ppermute | solution.py:39
  33.1 1.4 collective-permute-start.1
  34.5 2.4 collective-permute-done.1
  37.0 8.8 %collective-permute-start.2 = (s32[4,256]{1,0:T(4,128)S(1)}, s32[4,256]{1,0:T(4,128)S(1)}, u32[]{:S(2)}, u32[]{:S(2)}) collective-permute-start(s32[4,256]{1,0:T(4,128)S(1)} %fusion.64), channel_id=1, source_target_pairs={{0,32},{8,40},{16,48},{24,56},{32,0},{40,8},{48,16},{56,24},{1,33}... | collective-permute-start | bytes 12296 | tf_op jit(solution)/shard_map/ppermute | solution.py:39
  45.8 72.5 %collective-permute-done.2 = s32[4,256]{1,0:T(4,128)S(1)} collective-permute-done((s32[4,256]{1,0:T(4,128)S(1)}, s32[4,256]{1,0:T(4,128)S(1)}, u32[]{:S(2)}, u32[]{:S(2)}) %collective-permute-start.2) | collective-permute-done | bytes 4128 | tf_op jit(solution)/shard_map/ppermute | solution.py:39
  118.4 0.7 collective-permute-start.3
  119.0 3.9 %collective-permute-done.3 = s32[8,128]{1,0:T(8,128)S(1)} collective-permute-done((s32[8,128]{1,0:T(8,128)S(1)}, s32[8,128]{1,0:T(8,128)S(1)}, u32[]{:S(2)}, u32[]{:S(2)}) %collective-permute-start.3) | collective-permute-done | bytes 4128 | tf_op jit(solution)/shard_map/ppermute | solution.py:39
  123.1 0.5 collective-permute-start.4
  123.6 3.2 %collective-permute-done.4 = s32[16,64]{1,0:T(8,128)S(1)} collective-permute-done((s32[16,64]{1,0:T(8,128)S(1)}, s32[16,64]{1,0:T(8,128)S(1)}, u32[]{:S(2)}, u32[]{:S(2)}) %collective-permute-start.4) | collective-permute-done | bytes 4128 | tf_op jit(solution)/shard_map/ppermute | solution.py:39
  127.1 1.2 collective-permute-done.5
  128.5 2.3 collective-permute-start.6
  130.8 3.2 %collective-permute-done.6 = s32[64,16]{1,0:T(8,128)S(1)} collective-permute-done((s32[64,16]{1,0:T(8,128)S(1)}, s32[64,16]{1,0:T(8,128)S(1)}, u32[]{:S(2)}, u32[]{:S(2)}) %collective-permute-start.6) | collective-permute-done | bytes 4128 | tf_op jit(solution)/shard_map/ppermute | solution.py:39
  134.4 0.9 collective-permute-start.7
  135.3 3.7 %collective-permute-done.7 = s32[128,8]{1,0:T(8,128)S(1)} collective-permute-done((s32[128,8]{1,0:T(8,128)S(1)}, s32[128,8]{1,0:T(8,128)S(1)}, u32[]{:S(2)}, u32[]{:S(2)}) %collective-permute-start.7) | collective-permute-done | bytes 4128 | tf_op jit(solution)/shard_map/ppermute | solution.py:39
  140.1 0.6 select_reduce_fusion.2
  141.2 0.7 select_reduce_fusion.1
  141.9 5.5 %fusion.17 = bf16[512,1024]{1,0:T(8,128)(2,1)} fusion(bf16[256,8,1024]{2,1,0:T(8,128)(2,1)} %all-to-all-done, s32[2048]{0:T(1024)S(1)} %add_select_fusion.2), kind=kOutput, calls=%fused_computation.29 | convolution fusion | flops 2149056512 | bytes 5251072 | tf_op jit(solution)/shard_map/dot_general | solution.py:30
  147.4 4.5 %fusion.14 = bf16[512,1024]{1,0:T(8,128)(2,1)S(1)} fusion(bf16[256,8,1024]{2,1,0:T(8,128)(2,1)} %all-to-all-done, s32[2048]{0:T(1024)S(1)} %select_reduce_fusion.1), kind=kOutput, calls=%fused_computation.28 | convolution fusion | flops 2149056512 | bytes 5251072 | tf_op jit(solution)/shard_map/dot_general | solution.py:30
  152.1 1.3 all_to_all.25
  153.4 8.2 %all-to-all-start.1 = ((bf16[256,2,1152]{2,1,0:T(2,128)(2,1)}), bf16[256,2,1152]{2,1,0:T(2,128)(2,1)S(1)}, u32[]{:S(2)}, u32[]{:S(2)}) async-start(bf16[256,2,1152]{2,1,0:T(2,128)(2,1)} %all_to_all.25), calls=%async_computation.1 | async-start | bytes 2359296 | tf_op jit(solution)/shard_map/all_to_all | solution.py:99
  161.7 1.3 fusion.85
  162.9 1.3 fusion.86
  164.4 2.8 %fusion.20 = bf16[1024,512]{1,0:T(8,128)(2,1)S(1)} fusion(bf16[512,1024]{1,0:T(8,128)(2,1)} %collective-permute-done.8, bf16[512,1024]{1,0:T(8,128)(2,1)} %fusion.17, s32[512]{0:T(512)S(1)} %fusion.78), kind=kOutput, calls=%fused_computation.30 | convolution fusion | flops 1078984704 | bytes 3147776 | tf_op jit(solution)/shard_map/dot_general | solution.py:30
  167.2 1.3 fusion.48
  168.5 1.3 fusion.46
  169.8 1.3 fusion.44
  171.1 1.3 fusion.42
  172.4 23.9 %all-to-all-done.1 = bf16[256,2,1152]{2,1,0:T(2,128)(2,1)S(1)} async-done(((bf16[256,2,1152]{2,1,0:T(2,128)(2,1)}), bf16[256,2,1152]{2,1,0:T(2,128)(2,1)S(1)}, u32[]{:S(2)}, u32[]{:S(2)}) %all-to-all-start.1) | async-done | bytes 1179680 | tf_op jit(solution)/shard_map/all_to_all | solution.py:99
  196.3 1.3 all_to_all.27
  197.6 1.1 convert_reduce_fusion.2
  198.6 1.5 fusion.93
  200.4 1.8 collective-permute-done.9
  202.4 0.8 fusion.23
  203.4 0.4 fusion.28
  204.2 0.4 fusion.29
  204.7 0.6 copy-done.2
  205.3 0.4 fusion.30
  205.7 0.6 copy-done.1
  206.3 0.4 fusion.31
  206.9 18.0 %all_to_all.34 = bf16[4,512,256]{2,1,0:T(8,128)(2,1)S(1)} all-to-all(bf16[4,512,256]{2,1,0:T(8,128)(2,1)S(1)} %pad_maximum_fusion.2), channel_id=1, replica_groups=mesh['x'=4,'z'=8,'core'=2,'group'=4] {'group'}, dimensions={0} | all-to-all | bytes 2097152 | tf_op jit(solution)/shard_map/all_to_all | solution.py:140
  225.0 19.9 %all_to_all.35 = f32[32,16,256]{2,1,0:T(8,128)S(1)} all-to-all(f32[32,16,256]{2,1,0:T(8,128)S(1)} %bitcast.112), channel_id=1, replica_groups=mesh['x'=4,'z'=8,'core'=2,'group'=4] {'x','z'}, dimensions={0} | all-to-all | bytes 1048576 | tf_op jit(solution)/shard_map/all_to_all | solution.py:143
  245.0 0.6 broadcast_multiply_fusion
  (84 shorter events, 4.7 us)
Async XLA Ops:
  0.0 2.0 copy-start
  8.0 133.8 %all-to-all-start = ((bf16[256,8,1024]{2,1,0:T(8,128)(2,1)}), bf16[256,8,1024]{2,1,0:T(8,128)(2,1)}, u32[]{:S(2)}, u32[]{:S(2)}) async-start(bf16[256,8,1024]{2,1,0:T(8,128)(2,1)} %convert_bitcast_fusion), calls=%async_computation | async-start | bytes 8388608 | tf_op jit(solution)/shard_map/all_to_all | solution.py:78
  24.9 8.2 %collective-permute-start = (s32[1,1024]{1,0:T(1,128)S(1)}, s32[1,1024]{1,0:T(1,128)S(1)}, u32[]{:S(2)}, u32[]{:S(2)}) collective-permute-start(s32[1,1024]{1,0:T(1,128)S(1)} %fusion.61), channel_id=1, source_target_pairs={{0,128},{64,192},{128,0},{192,64},{1,129},{65,193},{129,1},{193,65... | collective-permute-start | bytes 12296 | tf_op jit(solution)/shard_map/ppermute | solution.py:39
  33.1 3.8 %collective-permute-start.1 = (s32[2,512]{1,0:T(2,128)S(1)}, s32[2,512]{1,0:T(2,128)S(1)}, u32[]{:S(2)}, u32[]{:S(2)}) collective-permute-start(s32[2,512]{1,0:T(2,128)S(1)} %select_bitcast_fusion.15), channel_id=1, source_target_pairs={{0,64},{64,0},{128,192},{192,128},{1,65},{65,1},{129,193},{193,129... | collective-permute-start | bytes 12296 | tf_op jit(solution)/shard_map/ppermute | solution.py:39
  37.0 81.3 %collective-permute-start.2 = (s32[4,256]{1,0:T(4,128)S(1)}, s32[4,256]{1,0:T(4,128)S(1)}, u32[]{:S(2)}, u32[]{:S(2)}) collective-permute-start(s32[4,256]{1,0:T(4,128)S(1)} %fusion.64), channel_id=1, source_target_pairs={{0,32},{8,40},{16,48},{24,56},{32,0},{40,8},{48,16},{56,24},{1,33}... | collective-permute-start | bytes 12296 | tf_op jit(solution)/shard_map/ppermute | solution.py:39
  118.4 4.6 %collective-permute-start.3 = (s32[8,128]{1,0:T(8,128)S(1)}, s32[8,128]{1,0:T(8,128)S(1)}, u32[]{:S(2)}, u32[]{:S(2)}) collective-permute-start(s32[8,128]{1,0:T(8,128)S(1)} %select_bitcast_fusion.14), channel_id=1, source_target_pairs={{0,16},{8,24},{16,0},{24,8},{32,48},{40,56},{48,32},{56,40},{1,17}... | collective-permute-start | bytes 12296 | tf_op jit(solution)/shard_map/ppermute | solution.py:39
  123.1 3.7 %collective-permute-start.4 = (s32[16,64]{1,0:T(8,128)S(1)}, s32[16,64]{1,0:T(8,128)S(1)}, u32[]{:S(2)}, u32[]{:S(2)}) collective-permute-start(s32[16,64]{1,0:T(8,128)S(1)} %select_bitcast_fusion.11), channel_id=1, source_target_pairs={{0,8},{8,0},{16,24},{24,16},{32,40},{40,32},{48,56},{56,48},{1,9},... | collective-permute-start | bytes 12296 | tf_op jit(solution)/shard_map/ppermute | solution.py:39
  127.0 1.3 collective-permute-start.5
  128.5 5.5 %collective-permute-start.6 = (s32[64,16]{1,0:T(8,128)S(1)}, s32[64,16]{1,0:T(8,128)S(1)}, u32[]{:S(2)}, u32[]{:S(2)}) collective-permute-start(s32[64,16]{1,0:T(8,128)S(1)} %select_bitcast_fusion.5), channel_id=1, source_target_pairs={{0,2},{1,3},{2,0},{3,1},{4,6},{5,7},{6,4},{7,5},{8,10},{9,11},{10,... | collective-permute-start | bytes 12296 | tf_op jit(solution)/shard_map/ppermute | solution.py:39
  134.4 4.5 %collective-permute-start.7 = (s32[128,8]{1,0:T(8,128)S(1)}, s32[128,8]{1,0:T(8,128)S(1)}, u32[]{:S(2)}, u32[]{:S(2)}) collective-permute-start(s32[128,8]{1,0:T(8,128)S(1)} %select_bitcast_fusion.2), channel_id=1, source_target_pairs={{0,1},{1,0},{2,3},{3,2},{4,5},{5,4},{6,7},{7,6},{8,9},{9,8},{10,11... | collective-permute-start | bytes 12296 | tf_op jit(solution)/shard_map/ppermute | solution.py:39
  147.4 15.6 %collective-permute-start.8 = (bf16[512,1024]{1,0:T(8,128)(2,1)}, bf16[512,1024]{1,0:T(8,128)(2,1)}, u32[]{:S(2)}, u32[]{:S(2)}) collective-permute-start(bf16[512,1024]{1,0:T(8,128)(2,1)} %fusion.17), channel_id=1, source_target_pairs={{0,4},{4,0},{1,5},{5,1},{2,6},{6,2},{3,7},{7,3},{8,12},{12,8},{9,1... | collective-permute-start | bytes 3145736 | tf_op jit(solution)/shard_map/ppermute | solution.py:39
  153.4 42.9 %all-to-all-start.1 = ((bf16[256,2,1152]{2,1,0:T(2,128)(2,1)}), bf16[256,2,1152]{2,1,0:T(2,128)(2,1)S(1)}, u32[]{:S(2)}, u32[]{:S(2)}) async-start(bf16[256,2,1152]{2,1,0:T(2,128)(2,1)} %all_to_all.25), calls=%async_computation.1 | async-start | bytes 2359296 | tf_op jit(solution)/shard_map/all_to_all | solution.py:99
  200.3 2.0 collective-permute-start.9
  202.3 1.0 copy-start.4
  203.1 1.1 copy-start.3
  204.2 1.0 copy-start.2
  205.3 1.0 copy-start.1

commit v3 on v2

--- a/solution.py
+++ b/solution.py
@@ -40,10 +40,12 @@
 
 
 def exchange(blocks):
-    classes, k = blocks.shape
-    held = blocks.reshape(-1)
-    before = 1
-    for axis in AXES:
+    k = blocks.shape[1]
+    sizes = [lax.axis_size(axis) for axis in AXES]
+    held = blocks.reshape(*sizes, k).transpose(1, 0, 2, 3, 4).reshape(sizes[1], -1)
+    held = lax.all_to_all(held, "z", 0, 0, tiled=True).reshape(-1)
+    before = sizes[1]
+    for axis in ("x", "core", "group"):
         bit = lax.axis_size(axis) // 2
         while bit:
             view = held.reshape(before, 2, -1)
@@ -56,14 +58,15 @@
             held = jnp.stack([low_part, high_part], axis=1).reshape(-1)
             before *= 2
             bit //= 2
-    return held.reshape(classes, k)
+    held = held.reshape(sizes[1], sizes[0], -1).transpose(1, 0, 2)
+    return held.reshape(-1)
 
 
 def solution(mesh):
     row_count, group_count = mesh.shape["rows"], mesh.shape["group"]
     classes = row_count * group_count
-    planes = row_count // 2
-    fine = Mesh(mesh.devices.reshape(4, row_count // 8, 2, group_count), AXES)
+    x_count, z_count = 4, row_count // 8
+    fine = Mesh(mesh.devices.reshape(x_count, z_count, 2, group_count), AXES)
     workers_here = WORKERS // classes
     firms_here = FIRMS // classes
 
@@ -78,7 +81,7 @@
         got = lax.all_to_all(packed, EVERYONE, 0, 0, tiled=True)
         code = (worker_ids // classes) * FIRMS + firm_ids
         slot_codes = placed_values(target, code, classes * capacity)
-        codes = exchange(slot_codes.reshape(classes, capacity)).reshape(-1)
+        codes = exchange(slot_codes.reshape(classes, capacity))
 
         used = codes >= 0
         worker = jnp.where(used, codes // FIRMS, -1)
@@ -100,11 +103,14 @@
             jnp.concatenate([sent, tail], axis=1), EVERYONE, 0, 0, tiled=True
         )
 
-        pairs = dot(one_hot(pair, 2 * workers_here), got).astype(jnp.bfloat16)
-        more = swapped(pairs, "core", 1)
         half = workers_here
-        left = jnp.concatenate([pairs, more], axis=0)
-        right = jnp.concatenate([pairs[half:], pairs[:half], more[half:], more[:half]], axis=0)
+        other_slot = jnp.concatenate([pair_slot[half:], pair_slot[:half]])
+        slots = jnp.arange(2 * classes, dtype=jnp.int32)
+        has_pair = slots[:, None] == jnp.where(pair_slot >= 0, pair_slot, -1)[None, :]
+        partner = jnp.max(jnp.where(has_pair, other_slot[None, :], -1), axis=1)
+        mates = dot((partner[:, None] == slots[None, :]).astype(jnp.bfloat16), sent).astype(jnp.bfloat16)
+        left = jnp.concatenate([sent, swapped(sent, "core", 1)], axis=0)
+        right = jnp.concatenate([mates, swapped(mates, "core", 1)], axis=0)
         block_rows, block_cols = width // row_count, width // group_count
         picked = jnp.arange(width // 2, dtype=jnp.int32)
         picked = (picked // block_rows * 2 + core) * block_rows + picked % block_rows
@@ -129,21 +135,20 @@
              firm_pair[n : 2 * n], firm_pair[3 * n :]],
             axis=0,
         )
-        terms = jnp.stack(
-            [
-                (worker_terms[g] + gram(firm_left, firm_right[:, g * block_cols : (g + 1) * block_cols])).astype(
-                    jnp.bfloat16
-                )
-                for g in range(group_count)
-            ]
-        )
-        terms = lax.all_to_all(terms, "group", 0, 0, tiled=True)
-        wide = [terms[g].astype(jnp.float32) for g in range(group_count)]
+        terms = [
+            (worker_terms[g] + gram(firm_left, firm_right[:, g * block_cols : (g + 1) * block_cols]))
+            .astype(jnp.bfloat16)
+            .reshape(x_count, -1, block_cols)
+            for g in range(group_count)
+        ]
+        terms = jnp.stack(terms, axis=1).reshape(x_count * group_count, -1, block_cols)
+        terms = lax.all_to_all(terms, ("x", "group"), 0, 0, tiled=True)
+        wide = [terms[i].astype(jnp.float32) for i in range(x_count * group_count)]
         terms = sum(wide[1:], wide[0])
         terms = lax.all_to_all(
-            terms.reshape(planes, block_rows, block_cols), ("x", "z"), 0, 0, tiled=True
+            terms.reshape(z_count, block_rows, block_cols), "z", 0, 0, tiled=True
         )
-        total = jnp.sum(terms, axis=0)
+        total = sum([terms[i] for i in range(1, z_count)], terms[0])
         return total * (1.0 / (classes * local_rows))
 
     placed = (P(EVERYONE, None), P(EVERYONE), P(EVERYONE))

time: 248 us -> 225 us (0.907)
  starting transfers between devices: 41.6 us -> 35.4 us
  waiting for transfers between devices: 121 us -> 115 us
  blocking collectives: 37.9 us -> 32 us
  matrix products: 28 us -> 25.5 us
    ppermute x10 -> x8, waiting for transfers between devices: 97 us -> 20.3 us  [swapped(): return lax.ppermute(value, axis, [(i, i ^ bit) for i in range(size)])]
    all_to_all x1, waiting for transfers between devices: 0.01 us -> 68.5 us  [local(): got = lax.all_to_all(packed, EVERYONE, 0, 0, tiled=True)]
    ppermute x10 -> x8, starting transfers between devices: 17.8 us -> 7.78 us  [swapped(): return lax.ppermute(value, axis, [(i, i ^ bit) for i in range(size)])]
    all_to_all x0 -> x1, starting transfers between devices: none -> 8.47 us  [exchange(): held = lax.all_to_all(held, 'z', 0, 0, tiled=True).reshape(-1)]
    all_to_all x2, blocking collectives: 37.9 us -> 32 us  [the longest x1 20.6 us: local(): terms = lax.all_to_all(terms, ('x', 'group'), 0, 0, tiled=True)]
    all_to_all x1, starting transfers between devices: 15.6 us -> 12.6 us  [local(): got = lax.all_to_all(packed, EVERYONE, 0, 0, tiled=True)]
    slice x2, local copies, waits for them, and re-layouts: 2.54 us -> 0.01 us  [the longest x1 0.01 us: local(): wide = [terms[i].astype(jnp.float32) for i in range(x_count * group_count)]]
    dot_general x6, matrix products: 21.2 us -> 18.6 us  [dot(): return jnp.dot(a, b, preferred_element_type=jnp.float32)]
  transfers between devices with their start and end apart: 12 -> 11, of which waited for: 10 -> 9; matrix products, arithmetic and copies ran while one was open for 8% -> 10% of each run, Pallas kernels for 0% -> 0%
where the time goes in v3:
time: 225 us
  waiting for transfers between devices  115 us (51%)
  starting transfers between devices  35.4 us (16%)
  blocking collectives  32 us (14%)
  matrix products  25.5 us (11%)
  other arithmetic  9.62 us (4%)
  local copies, waits for them, and re-layouts  6.89 us (3%)
    all_to_all x1, waiting for transfers between devices, local(): got = lax.all_to_all(packed, EVERYONE, 0, 0, tiled=True)  68.5 us
    all_to_all x1, waiting for transfers between devices, local(): lax.all_to_all(jnp.concatenate([sent, tail], axis=1), EVERYONE, 0, 0, til...  24.3 us
    all_to_all x1, blocking collectives, local(): terms = lax.all_to_all(terms, ('x', 'group'), 0, 0, tiled=True)  20.6 us
    ppermute x8, waiting for transfers between devices, swapped(): return lax.ppermute(value, axis, [(i, i ^ bit) for i in range(size)])  20.3 us
    dot_general x6, matrix products, dot(): return jnp.dot(a, b, preferred_element_type=jnp.float32)  18.6 us
    all_to_all x1, starting transfers between devices, local(): got = lax.all_to_all(packed, EVERYONE, 0, 0, tiled=True)  12.6 us
    all_to_all x1, blocking collectives, local(): lax.all_to_all(terms.reshape(z_count, block_rows, block_cols), 'z', 0, 0,...  11.5 us
    all_to_all x1, starting transfers between devices, exchange(): held = lax.all_to_all(held, 'z', 0, 0, tiled=True).reshape(-1)  8.47 us
  transfers between devices with their start and end apart: 11, of which 9 were waited for; matrix products, arithmetic and copies ran while one was open for 10% of the time, Pallas kernels for 0%

profile of v3, /device:TPU:8, one launch (start us, length us, event | category | flops | bytes accessed | tf_op | source)
XLA Modules:
  0.0 224.6 jit_solution(6719593240317642275)
XLA Ops:
  0.0 0.8 add_select_fusion.4
  0.8 0.4 convert_reduce_fusion
  1.3 0.7 multiply_add_fusion
  2.0 1.2 select_reduce_fusion
  3.4 0.8 all_to_all.38
  4.2 8.5 %all-to-all-start = ((s32[8,1,256]{2,1,0:T(1,128)}), s32[8,1,256]{2,1,0:T(1,128)S(1)}, u32[]{:S(2)}, u32[]{:S(2)}) async-start(s32[8,1,256]{2,1,0:T(1,128)} %all_to_all.38), calls=%async_computation | async-start | bytes 16384 | tf_op jit(solution)/shard_map/all_to_all | solution.py:46
  12.6 6.0 %convert_bitcast_fusion = bf16[256,8,1024]{2,1,0:T(8,128)(2,1)} fusion(bf16[1024,1024]{1,0:T(8,128)(2,1)S(1)} %copy-done, s32[1024]{0:T(1024)S(1)} %get-tuple-element.43), kind=kOutput, calls=%fused_computation.5 | convolution fusion | flops 4299161600 | bytes 6295552 | tf_op jit(solution)/shard_map/dot_general | solution.py:30
  18.7 1.7 all-to-all-done
  20.3 12.6 %all-to-all-start.1 = ((bf16[256,8,1024]{2,1,0:T(8,128)(2,1)}), bf16[256,8,1024]{2,1,0:T(8,128)(2,1)}, u32[]{:S(2)}, u32[]{:S(2)}) async-start(bf16[256,8,1024]{2,1,0:T(8,128)(2,1)} %convert_bitcast_fusion), calls=%async_computation.1 | async-start | bytes 8388608 | tf_op jit(solution)/shard_map/all_to_all | solution.py:81
  33.0 3.1 %collective-permute-start = (s32[8,128]{1,0:T(8,128)S(1)}, s32[8,128]{1,0:T(8,128)S(1)}, u32[]{:S(2)}, u32[]{:S(2)}) collective-permute-start(s32[8,128]{1,0:T(8,128)S(1)} %select_bitcast_fusion.12), channel_id=1, source_target_pairs={{0,128},{64,192},{128,0},{192,64},{1,129},{65,193},{129,1},{193,65... | collective-permute-start | bytes 12296 | tf_op jit(solution)/shard_map/ppermute | solution.py:39
  36.1 6.3 %collective-permute-done = s32[8,128]{1,0:T(8,128)S(1)} collective-permute-done((s32[8,128]{1,0:T(8,128)S(1)}, s32[8,128]{1,0:T(8,128)S(1)}, u32[]{:S(2)}, u32[]{:S(2)}) %collective-permute-start) | collective-permute-done | bytes 4128 | tf_op jit(solution)/shard_map/ppermute | solution.py:39
  42.5 1.4 collective-permute-start.1
  43.9 2.4 %collective-permute-done.1 = s32[16,64]{1,0:T(8,128)S(1)} collective-permute-done((s32[16,64]{1,0:T(8,128)S(1)}, s32[16,64]{1,0:T(8,128)S(1)}, u32[]{:S(2)}, u32[]{:S(2)}) %collective-permute-start.1) | collective-permute-done | bytes 4128 | tf_op jit(solution)/shard_map/ppermute | solution.py:39
  46.6 1.2 collective-permute-done.2
  48.0 2.4 %collective-permute-start.3 = (s32[64,16]{1,0:T(8,128)S(1)}, s32[64,16]{1,0:T(8,128)S(1)}, u32[]{:S(2)}, u32[]{:S(2)}) collective-permute-start(s32[64,16]{1,0:T(8,128)S(1)} %select_bitcast_fusion.5), channel_id=1, source_target_pairs={{0,2},{1,3},{2,0},{3,1},{4,6},{5,7},{6,4},{7,5},{8,10},{9,11},{10,... | collective-permute-start | bytes 12296 | tf_op jit(solution)/shard_map/ppermute | solution.py:39
  50.4 3.6 %collective-permute-done.3 = s32[64,16]{1,0:T(8,128)S(1)} collective-permute-done((s32[64,16]{1,0:T(8,128)S(1)}, s32[64,16]{1,0:T(8,128)S(1)}, u32[]{:S(2)}, u32[]{:S(2)}) %collective-permute-start.3) | collective-permute-done | bytes 4128 | tf_op jit(solution)/shard_map/ppermute | solution.py:39
  54.7 5.0 %collective-permute-done.4 = s32[128,8]{1,0:T(8,128)S(1)} collective-permute-done((s32[128,8]{1,0:T(8,128)S(1)}, s32[128,8]{1,0:T(8,128)S(1)}, u32[]{:S(2)}, u32[]{:S(2)}) %collective-permute-start.4) | collective-permute-done | bytes 4128 | tf_op jit(solution)/shard_map/ppermute | solution.py:39
  60.5 0.4 select_reduce_fusion.3
  60.9 0.6 select_reduce_fusion.2
  62.2 0.7 select_reduce_fusion.1
  62.9 68.5 %all-to-all-done.1 = bf16[256,8,1024]{2,1,0:T(8,128)(2,1)} async-done(((bf16[256,8,1024]{2,1,0:T(8,128)(2,1)}), bf16[256,8,1024]{2,1,0:T(8,128)(2,1)}, u32[]{:S(2)}, u32[]{:S(2)}) %all-to-all-start.1) | async-done | bytes 4194336 | tf_op jit(solution)/shard_map/all_to_all | solution.py:81
  131.4 5.5 %fusion.11 = bf16[512,1024]{1,0:T(8,128)(2,1)} fusion(bf16[256,8,1024]{2,1,0:T(8,128)(2,1)} %all-to-all-done.1, s32[2048]{0:T(1024)S(1)} %select_reduce_fusion.1), kind=kOutput, calls=%fused_computation.30 | convolution fusion | flops 2149056512 | bytes 5251072 | tf_op jit(solution)/shard_map/dot_general | solution.py:30
  137.0 1.3 pad_maximum_fusion
  138.3 1.3 all_to_all.33
  139.7 6.5 %all-to-all-start.2 = ((bf16[256,2,1152]{2,1,0:T(2,128)(2,1)}), bf16[256,2,1152]{2,1,0:T(2,128)(2,1)S(1)}, u32[]{:S(2)}, u32[]{:S(2)}) async-start(bf16[256,2,1152]{2,1,0:T(2,128)(2,1)} %all_to_all.33), calls=%async_computation.2 | async-start | bytes 2359296 | tf_op jit(solution)/shard_map/all_to_all | solution.py:102
  146.1 2.0 convolution_convert_fusion
  148.1 0.5 collective-permute-start.6
  148.6 2.8 %fusion.14 = bf16[1024,512]{1,0:T(8,128)(2,1)S(1)} fusion(bf16[512,1024]{1,0:T(8,128)(2,1)} %collective-permute-done.5, bf16[512,1024]{1,0:T(8,128)(2,1)} %fusion.11, s32[512]{0:T(512)S(1)} %fusion.69), kind=kOutput, calls=%fused_computation.31 | convolution fusion | flops 1078984704 | bytes 3147776 | tf_op jit(solution)/shard_map/dot_general | solution.py:30
  151.5 1.3 fusion.41
  152.8 1.3 fusion.33
  154.0 1.3 fusion.39
  155.3 1.3 fusion.36
  156.6 24.3 %all-to-all-done.2 = bf16[256,2,1152]{2,1,0:T(2,128)(2,1)S(1)} async-done(((bf16[256,2,1152]{2,1,0:T(2,128)(2,1)}), bf16[256,2,1152]{2,1,0:T(2,128)(2,1)S(1)}, u32[]{:S(2)}, u32[]{:S(2)}) %all-to-all-start.2) | async-done | bytes 1179680 | tf_op jit(solution)/shard_map/all_to_all | solution.py:102
  180.9 1.3 all_to_all.35
  182.2 1.1 convert_reduce_fusion.2
  183.2 1.5 fusion.86
  185.0 1.8 collective-permute-done.7
  186.9 0.8 fusion.17
  187.8 0.9 copy-done.4
  188.7 0.4 fusion.18
  189.1 0.4 fusion.19
  189.6 0.6 copy-done.2
  190.2 0.4 fusion.20
  190.6 0.6 copy-done.1
  191.2 0.4 fusion.21
  191.8 20.6 %all_to_all.44 = bf16[16,128,256]{2,1,0:T(8,128)(2,1)S(1)} all-to-all(bf16[16,128,256]{2,1,0:T(8,128)(2,1)S(1)} %bitcast.93), channel_id=1, replica_groups=mesh['x'=4,'z'=8,'core'=2,'group'=4] {'x','group'}, dimensions={0} | all-to-all | bytes 2097152 | tf_op jit(solution)/shard_map/all_to_all | solution.py:145
  212.5 11.5 %all_to_all.45 = f32[8,16,256]{2,1,0:T(8,128)S(1)} all-to-all(f32[8,16,256]{2,1,0:T(8,128)S(1)} %convert_add_fusion), channel_id=1, replica_groups=mesh['x'=4,'z'=8,'core'=2,'group'=4] {'z'}, dimensions={0} | all-to-all | bytes 262144 | tf_op jit(solution)/shard_map/all_to_all | solution.py:148
  224.0 0.6 fusion.50
  (73 shorter events, 3.7 us)
Async XLA Ops:
  0.0 12.6 %copy-start = (bf16[1024,1024]{1,0:T(8,128)(2,1)S(1)}, bf16[1024,1024]{1,0:T(8,128)(2,1)}, u32[]{:S(2)}) copy-start(bf16[1024,1024]{1,0:T(8,128)(2,1)} %param.3) | copy-start | bytes 6291460
  4.2 16.2 %all-to-all-start = ((s32[8,1,256]{2,1,0:T(1,128)}), s32[8,1,256]{2,1,0:T(1,128)S(1)}, u32[]{:S(2)}, u32[]{:S(2)}) async-start(s32[8,1,256]{2,1,0:T(1,128)} %all_to_all.38), calls=%async_computation | async-start | bytes 16384 | tf_op jit(solution)/shard_map/all_to_all | solution.py:46
  20.3 111.0 %all-to-all-start.1 = ((bf16[256,8,1024]{2,1,0:T(8,128)(2,1)}), bf16[256,8,1024]{2,1,0:T(8,128)(2,1)}, u32[]{:S(2)}, u32[]{:S(2)}) async-start(bf16[256,8,1024]{2,1,0:T(8,128)(2,1)} %convert_bitcast_fusion), calls=%async_computation.1 | async-start | bytes 8388608 | tf_op jit(solution)/shard_map/all_to_all | solution.py:81
  33.0 9.4 %collective-permute-start = (s32[8,128]{1,0:T(8,128)S(1)}, s32[8,128]{1,0:T(8,128)S(1)}, u32[]{:S(2)}, u32[]{:S(2)}) collective-permute-start(s32[8,128]{1,0:T(8,128)S(1)} %select_bitcast_fusion.12), channel_id=1, source_target_pairs={{0,128},{64,192},{128,0},{192,64},{1,129},{65,193},{129,1},{193,65... | collective-permute-start | bytes 12296 | tf_op jit(solution)/shard_map/ppermute | solution.py:39
  42.5 3.8 %collective-permute-start.1 = (s32[16,64]{1,0:T(8,128)S(1)}, s32[16,64]{1,0:T(8,128)S(1)}, u32[]{:S(2)}, u32[]{:S(2)}) collective-permute-start(s32[16,64]{1,0:T(8,128)S(1)} %select_bitcast_fusion.11), channel_id=1, source_target_pairs={{0,64},{64,0},{128,192},{192,128},{1,65},{65,1},{129,193},{193,129... | collective-permute-start | bytes 12296 | tf_op jit(solution)/shard_map/ppermute | solution.py:39
  46.5 1.3 collective-permute-start.2
  48.0 6.0 %collective-permute-start.3 = (s32[64,16]{1,0:T(8,128)S(1)}, s32[64,16]{1,0:T(8,128)S(1)}, u32[]{:S(2)}, u32[]{:S(2)}) collective-permute-start(s32[64,16]{1,0:T(8,128)S(1)} %select_bitcast_fusion.5), channel_id=1, source_target_pairs={{0,2},{1,3},{2,0},{3,1},{4,6},{5,7},{6,4},{7,5},{8,10},{9,11},{10,... | collective-permute-start | bytes 12296 | tf_op jit(solution)/shard_map/ppermute | solution.py:39
  54.4 5.3 %collective-permute-start.4 = (s32[128,8]{1,0:T(8,128)S(1)}, s32[128,8]{1,0:T(8,128)S(1)}, u32[]{:S(2)}, u32[]{:S(2)}) collective-permute-start(s32[128,8]{1,0:T(8,128)S(1)} %select_bitcast_fusion.2), channel_id=1, source_target_pairs={{0,1},{1,0},{2,3},{3,2},{4,5},{5,4},{6,7},{7,6},{8,9},{9,8},{10,11... | collective-permute-start | bytes 12296 | tf_op jit(solution)/shard_map/ppermute | solution.py:39
  136.9 11.7 %collective-permute-start.5 = (bf16[512,1024]{1,0:T(8,128)(2,1)}, bf16[512,1024]{1,0:T(8,128)(2,1)}, u32[]{:S(2)}, u32[]{:S(2)}) collective-permute-start(bf16[512,1024]{1,0:T(8,128)(2,1)} %fusion.11), channel_id=1, source_target_pairs={{0,4},{4,0},{1,5},{5,1},{2,6},{6,2},{3,7},{7,3},{8,12},{12,8},{9,1... | collective-permute-start | bytes 3145736 | tf_op jit(solution)/shard_map/ppermute | solution.py:39
  139.7 41.2 %all-to-all-start.2 = ((bf16[256,2,1152]{2,1,0:T(2,128)(2,1)}), bf16[256,2,1152]{2,1,0:T(2,128)(2,1)S(1)}, u32[]{:S(2)}, u32[]{:S(2)}) async-start(bf16[256,2,1152]{2,1,0:T(2,128)(2,1)} %all_to_all.33), calls=%async_computation.2 | async-start | bytes 2359296 | tf_op jit(solution)/shard_map/all_to_all | solution.py:102
  148.1 3.3 %collective-permute-start.6 = (bf16[512,1024]{1,0:T(8,128)(2,1)S(1)}, bf16[512,1024]{1,0:T(8,128)(2,1)S(1)}, u32[]{:S(2)}, u32[]{:S(2)}) collective-permute-start(bf16[512,1024]{1,0:T(8,128)(2,1)S(1)} %convolution_convert_fusion), channel_id=1, source_target_pairs={{0,4},{4,0},{1,5},{5,1},{2,6},{6,2},{3,7},{7,3},{8,12},{12,8},{9,1... | collective-permute-start | bytes 3145736 | tf_op jit(solution)/shard_map/ppermute | solution.py:39
  184.9 2.0 collective-permute-start.7
  187.7 1.0 copy-start.4
  187.8 1.3 copy-start.3
  189.1 1.0 copy-start.2
  190.2 1.0 copy-start.1

commit v4 on v3

--- a/solution.py
+++ b/solution.py
@@ -1,11 +1,13 @@
 import jax
 import jax.numpy as jnp
 from jax import lax
+from jax.experimental import pallas as pl
+from jax.experimental.pallas import tpu as pltpu
 from jax.sharding import Mesh, PartitionSpec as P
 
+LANES = 128
 AXES = ("x", "z", "core", "group")
 EVERYONE = AXES
-LANES = 128
 FIRMS = 32768
 WORKERS = 65536
 
@@ -39,12 +41,8 @@
     return lax.ppermute(value, axis, [(i, i ^ bit) for i in range(size)])
 
 
-def exchange(blocks):
-    k = blocks.shape[1]
-    sizes = [lax.axis_size(axis) for axis in AXES]
-    held = blocks.reshape(*sizes, k).transpose(1, 0, 2, 3, 4).reshape(sizes[1], -1)
-    held = lax.all_to_all(held, "z", 0, 0, tiled=True).reshape(-1)
-    before = sizes[1]
+def swap_bits(held, before):
+    shape = held.shape
     for axis in ("x", "core", "group"):
         bit = lax.axis_size(axis) // 2
         while bit:
@@ -55,11 +53,59 @@
             came = swapped(send, axis, bit)
             low_part = jnp.where(high, came, keep)
             high_part = jnp.where(high, keep, came)
-            held = jnp.stack([low_part, high_part], axis=1).reshape(-1)
+            held = jnp.stack([low_part, high_part], axis=1)
             before *= 2
             bit //= 2
-    held = held.reshape(sizes[1], sizes[0], -1).transpose(1, 0, 2)
-    return held.reshape(-1)
+    return held.reshape(shape)
+
+
+def all_terms(own, other, pick, worker_terms, row_parts, col_parts):
+    firms, width = own.shape[0] // 2, own.shape[1]
+    picked = pick.shape[0]
+    cols = width // col_parts
+
+    def kernel(own_ref, other_ref, pick_ref, terms_ref, out_ref, high_ref, low_ref, left_ref):
+        g = pl.program_id(0)
+
+        @pl.when(g == 0)
+        def _():
+            high_ref[:firms] = own_ref[:firms]
+            high_ref[firms:] = other_ref[:firms]
+            low_ref[:firms] = own_ref[firms:]
+            low_ref[firms:] = other_ref[firms:]
+            across = (((1,), (1,)), ((), ()))
+            for at, ref in ((0, high_ref), (2 * firms, low_ref)):
+                left_ref[:, at : at + 2 * firms] = lax.dot_general(
+                    pick_ref[...], ref[...], across, preferred_element_type=jnp.float32
+                ).astype(jnp.bfloat16)
+
+        here = pl.ds(pl.multiple_of(g * cols, cols), cols)
+        high, low = high_ref[:, here], low_ref[:, here]
+        left_high, left_low = left_ref[:, : 2 * firms], left_ref[:, 2 * firms :]
+        sums = terms_ref[...] + (dot(left_high, low) + dot(left_low, high)) + dot(left_high, high)
+        out_ref[...] = sums.astype(jnp.bfloat16).reshape(out_ref.shape)
+
+    return pl.pallas_call(
+        kernel,
+        grid=(col_parts,),
+        in_specs=[
+            pl.BlockSpec((2 * firms, width), lambda g: (0, 0)),
+            pl.BlockSpec((2 * firms, width), lambda g: (0, 0)),
+            pl.BlockSpec((picked, width), lambda g: (0, 0)),
+            pl.BlockSpec((picked, cols), lambda g: (0, g)),
+        ],
+        out_specs=pl.BlockSpec((row_parts, 1, picked // row_parts, cols), lambda g: (0, g, 0, 0)),
+        out_shape=jax.ShapeDtypeStruct((row_parts, col_parts, picked // row_parts, cols), jnp.bfloat16),
+        scratch_shapes=[
+            pltpu.VMEM((2 * firms, width), jnp.bfloat16),
+            pltpu.VMEM((2 * firms, width), jnp.bfloat16),
+            pltpu.VMEM((picked, 4 * firms), jnp.bfloat16),
+        ],
+        compiler_params=pltpu.CompilerParams(vmem_limit_bytes=24 * 1024 * 1024),
+        cost_estimate=pl.CostEstimate(
+            flops=2 * picked * width * 10 * firms, bytes_accessed=6 * 1024 * 1024, transcendentals=0
+        ),
+    )(own, other, pick, worker_terms)
 
 
 def solution(mesh):
@@ -75,13 +121,28 @@
         capacity = 2 * local_rows // classes
         core = lax.axis_index("core")
 
+        raw = worker_ids * FIRMS + firm_ids
+        raw = lax.all_to_all(
+            jnp.broadcast_to(raw[None, :], (z_count, local_rows)), "z", 0, 0, tiled=True
+        )
+
         home = worker_ids % classes
         target = home * capacity + equal_before(home)
         packed = dot(one_hot(target, classes * capacity), scores).astype(jnp.bfloat16)
+        packed, raw = lax.optimization_barrier((packed, raw))
         got = lax.all_to_all(packed, EVERYONE, 0, 0, tiled=True)
-        code = (worker_ids // classes) * FIRMS + firm_ids
-        slot_codes = placed_values(target, code, classes * capacity)
-        codes = exchange(slot_codes.reshape(classes, capacity))
+
+        inner = 2 * group_count
+        raw_worker = raw // FIRMS
+        raw_home = raw_worker % classes
+        mine = (raw_home // inner) % z_count == lax.axis_index("z")
+        across = (raw_home // (inner * z_count)) * inner + raw_home % inner
+        across = jnp.where(mine, across, -1)
+        slot = jnp.where(mine, across * capacity + jax.vmap(equal_before)(across), -1)
+        raw_code = (raw_worker // classes) * FIRMS + raw % FIRMS
+        slot_codes = jax.vmap(lambda t, v: placed_values(t, v, x_count * inner * capacity))(slot, raw_code)
+        codes = swap_bits(slot_codes, z_count)
+        codes = codes.reshape(z_count, x_count, -1).transpose(1, 0, 2).reshape(-1)
 
         used = codes >= 0
         worker = jnp.where(used, codes // FIRMS, -1)
@@ -97,7 +158,8 @@
         row_slot = jnp.max(jnp.where(pair_rows == pair[None, :], pair_slot[:, None], -1), axis=0)
         sent_firm = placed_values(pair_slot, pair_firm // classes, 2 * classes)
 
-        sent = dot(one_hot(row_slot, 2 * classes), got).astype(jnp.bfloat16)
+        to_slots, got = lax.optimization_barrier((one_hot(row_slot, 2 * classes), got))
+        sent = dot(to_slots, got).astype(jnp.bfloat16)
         tail = jnp.broadcast_to(sent_firm.astype(jnp.bfloat16)[:, None], (2 * classes, LANES))
         came = lax.all_to_all(
             jnp.concatenate([sent, tail], axis=1), EVERYONE, 0, 0, tiled=True
@@ -114,34 +176,24 @@
         block_rows, block_cols = width // row_count, width // group_count
         picked = jnp.arange(width // 2, dtype=jnp.int32)
         picked = (picked // block_rows * 2 + core) * block_rows + picked % block_rows
-        pick = one_hot(picked, width)
-        left = dot(left, pick).astype(jnp.bfloat16)
-        worker_terms = [
-            gram(left, right[:, g * block_cols : (g + 1) * block_cols]) for g in range(group_count)
-        ]
-
-        came, worker_terms = lax.optimization_barrier((came, worker_terms))
-        firm_local = came[:, width].astype(jnp.int32)
-        firm_sums = dot(one_hot(firm_local, firms_here), came[:, :width])
+        columns = jnp.arange(width, dtype=jnp.int32)
+        pick = (picked[:, None] == columns[None, :]).astype(jnp.bfloat16)
+        left = lax.dot_general(
+            left, pick, (((1,), (1,)), ((), ())), preferred_element_type=jnp.float32
+        ).astype(jnp.bfloat16)
+        worker_terms = gram(left, right)
+
+        came, worker_terms, pick = lax.optimization_barrier((came, worker_terms, pick))
+        firm_names = jnp.arange(firms_here, dtype=jnp.float32).astype(jnp.bfloat16)
+        firm_hits = (came[:, width:] == firm_names[None, :]).astype(jnp.bfloat16)
+        firm_sums = gram(firm_hits, came[:, :width])
         high = lax.optimization_barrier(firm_sums.astype(jnp.bfloat16))
         low = (firm_sums - high.astype(jnp.float32)).astype(jnp.bfloat16)
         firm_pair = jnp.concatenate([high, low], axis=0)
-        firm_pair = jnp.concatenate([firm_pair, swapped(firm_pair, "core", 1)], axis=0)
-        firm_left = dot(firm_pair, pick).astype(jnp.bfloat16)
-        n = firms_here
-        firm_left = jnp.concatenate([firm_left, firm_left[:n], firm_left[2 * n : 3 * n]], axis=0)
-        firm_right = jnp.concatenate(
-            [firm_pair[:n], firm_pair[:n], firm_pair[2 * n : 3 * n], firm_pair[2 * n : 3 * n],
-             firm_pair[n : 2 * n], firm_pair[3 * n :]],
-            axis=0,
-        )
-        terms = [
-            (worker_terms[g] + gram(firm_left, firm_right[:, g * block_cols : (g + 1) * block_cols]))
-            .astype(jnp.bfloat16)
-            .reshape(x_count, -1, block_cols)
-            for g in range(group_count)
-        ]
-        terms = jnp.stack(terms, axis=1).reshape(x_count * group_count, -1, block_cols)
+        terms = all_terms(
+            firm_pair, swapped(firm_pair, "core", 1), pick, worker_terms, x_count, group_count
+        )
+        terms = terms.reshape(x_count * group_count, -1, block_cols)
         terms = lax.all_to_all(terms, ("x", "group"), 0, 0, tiled=True)
         wide = [terms[i].astype(jnp.float32) for i in range(x_count * group_count)]
         terms = sum(wide[1:], wide[0])

time: 225 us -> 224 us (level)
  waiting for transfers between devices: 115 us -> 102 us
  other arithmetic: 9.62 us -> 18.4 us
  matrix products: 25.5 us -> 21.9 us
  starting transfers between devices: 35.4 us -> 38.8 us
  Pallas kernels: 0 us -> 2.54 us
    reduce_sum x2 -> x3, other arithmetic: 0.59 us -> 7.78 us  [equal_before(): return jnp.sum(same.astype(jnp.int32), axis=0)]
    all_to_all x1, waiting for transfers between devices: 68.5 us -> 61.6 us  [local(): got = lax.all_to_all(packed, EVERYONE, 0, 0, tiled=True)]
    dot_general x6 -> x3, matrix products: 18.6 us -> 14.1 us  [dot(): return jnp.dot(a, b, preferred_element_type=jnp.float32)]
    ppermute x8, waiting for transfers between devices: 20.3 us -> 16.8 us  [swapped(): return lax.ppermute(value, axis, [(i, i ^ bit) for i in range(size)])]
    all_to_all x1, waiting for transfers between devices: 24.3 us -> 21.1 us  [local(): lax.all_to_all(jnp.concatenate([sent, tail], axis=1), EVERYONE, 0, 0, til...]
    pallas_call x0 -> x1, Pallas kernels: none -> 2.54 us  [all_terms(): pl.pallas_call(kernel, grid=(col_parts,), in_specs=[pl.BlockSpec((2 * fir...]
    all_to_all x2, local copies, waits for them, and re-layouts: 2.6 us -> 4.99 us  [local(): lax.all_to_all(jnp.concatenate([sent, tail], axis=1), EVERYONE, 0, 0, til...]
    ppermute x8, starting transfers between devices: 7.78 us -> 10 us  [swapped(): return lax.ppermute(value, axis, [(i, i ^ bit) for i in range(size)])]
  transfers between devices with their start and end apart: 11 -> 11, of which waited for: 9 -> 11; matrix products, arithmetic and copies ran while one was open for 10% -> 13% of each run, Pallas kernels for 0% -> 0%
where the time goes in v4:
time: 224 us
  waiting for transfers between devices  102 us (46%)
  starting transfers between devices  38.8 us (17%)
  blocking collectives  32 us (14%)
  matrix products  21.9 us (10%)
  other arithmetic  18.4 us (8%)
  local copies, waits for them, and re-layouts  8.04 us (4%)
  Pallas kernels  2.54 us (1%)
    all_to_all x1, waiting for transfers between devices, local(): got = lax.all_to_all(packed, EVERYONE, 0, 0, tiled=True)  61.6 us
    all_to_all x1, waiting for transfers between devices, local(): lax.all_to_all(jnp.concatenate([sent, tail], axis=1), EVERYONE, 0, 0, til...  21.1 us
    all_to_all x1, blocking collectives, local(): terms = lax.all_to_all(terms, ('x', 'group'), 0, 0, tiled=True)  20.6 us
    ppermute x8, waiting for transfers between devices, swapped(): return lax.ppermute(value, axis, [(i, i ^ bit) for i in range(size)])  16.8 us
    dot_general x3, matrix products, dot(): return jnp.dot(a, b, preferred_element_type=jnp.float32)  14.1 us
    all_to_all x1, starting transfers between devices, local(): got = lax.all_to_all(packed, EVERYONE, 0, 0, tiled=True)  12.3 us
    all_to_all x1, blocking collectives, local(): lax.all_to_all(terms.reshape(z_count, block_rows, block_cols), 'z', 0, 0,...  11.5 us
    ppermute x8, starting transfers between devices, swapped(): return lax.ppermute(value, axis, [(i, i ^ bit) for i in range(size)])  10 us
  transfers between devices with their start and end apart: 11, of which 11 were waited for; matrix products, arithmetic and copies ran while one was open for 13% of the time, Pallas kernels for 0%

profile of v4, /device:TPU:8, one launch (start us, length us, event | category | flops | bytes accessed | tf_op | source)
XLA Modules:
  0.0 223.6 jit_solution(16932670368948808253)
XLA Ops:
  0.0 0.8 add_select_fusion.12
  0.8 0.4 convert_reduce_fusion.1
  1.3 0.7 multiply_add_fusion
  2.0 0.6 broadcast_in_dim.93
  2.6 8.5 %all-to-all-start = ((s32[8,1,1024]{2,1,0:T(1,128)}), s32[8,1,1024]{2,1,0:T(1,128)S(1)}, u32[]{:S(2)}, u32[]{:S(2)}) async-start(s32[8,1,1024]{2,1,0:T(1,128)} %broadcast_in_dim.93), calls=%async_computation | async-start | bytes 65536 | tf_op jit(solution)/shard_map/all_to_all | solution.py:125
  11.1 6.0 %fusion.3 = bf16[2048,1024]{1,0:T(8,128)(2,1)} fusion(bf16[1024,1024]{1,0:T(8,128)(2,1)S(1)} %copy-done, s32[1024]{0:T(1024)S(1)} %get-tuple-element.48), kind=kOutput, calls=%fused_computation.13 | convolution fusion | flops 4299161600 | bytes 6295552 | tf_op jit(solution)/shard_map/dot_general | solution.py:32
  17.1 2.0 all-to-all-done
  19.1 12.3 %all-to-all-start.1 = ((bf16[256,8,1024]{2,1,0:T(8,128)(2,1)}), bf16[256,8,1024]{2,1,0:T(8,128)(2,1)}, u32[]{:S(2)}, u32[]{:S(2)}) async-start(bf16[256,8,1024]{2,1,0:T(8,128)(2,1)} %bitcast.71), calls=%async_computation.1 | async-start | bytes 8388608 | tf_op jit(solution)/shard_map/all_to_all | solution.py:133
  31.5 0.3 iota_compare_fusion.3
  31.9 7.2 %convert_reduce_fusion = s32[8,1024]{1,0:T(8,128)S(1)} fusion(s32[8,1024]{1,0:T(8,128)S(1)} %fusion.31, pred[1024,1024]{1,0:T(8,128)(4,1)S(1)} %iota_compare_fusion.3), kind=kLoop, calls=%fused_computation | loop fusion | flops 33546240 | bytes 1114112 | tf_op jit(solution)/shard_map/vmap()/reduce_sum | solution.py:18
  39.2 1.2 select_reduce_fusion
  40.5 3.1 %collective-permute-start = (s32[8,128]{1,0:T(8,128)S(1)}, s32[8,128]{1,0:T(8,128)S(1)}, u32[]{:S(2)}, u32[]{:S(2)}) collective-permute-start(s32[8,128]{1,0:T(8,128)S(1)} %select_bitcast_fusion.12), channel_id=1, source_target_pairs={{0,128},{64,192},{128,0},{192,64},{1,129},{65,193},{129,1},{193,65... | collective-permute-start | bytes 12296 | tf_op jit(solution)/shard_map/ppermute | solution.py:41
  43.5 2.2 collective-permute-done
  45.8 1.5 collective-permute-start.1
  47.4 2.2 collective-permute-done.1
  49.9 1.2 collective-permute-done.2
  51.3 2.2 collective-permute-start.3
  53.5 3.5 %collective-permute-done.3 = s32[64,16]{1,0:T(8,128)S(1)} collective-permute-done((s32[64,16]{1,0:T(8,128)S(1)}, s32[64,16]{1,0:T(8,128)S(1)}, u32[]{:S(2)}, u32[]{:S(2)}) %collective-permute-start.3) | collective-permute-done | bytes 4128 | tf_op jit(solution)/shard_map/ppermute | solution.py:41
  57.4 2.5 %collective-permute-start.4 = (s32[128,8]{1,0:T(8,128)S(1)}, s32[128,8]{1,0:T(8,128)S(1)}, u32[]{:S(2)}, u32[]{:S(2)}) collective-permute-start(s32[128,8]{1,0:T(8,128)S(1)} %select_bitcast_fusion.2), channel_id=1, source_target_pairs={{0,1},{1,0},{2,3},{3,2},{4,5},{5,4},{6,7},{7,6},{8,9},{9,8},{10,11... | collective-permute-start | bytes 12296 | tf_op jit(solution)/shard_map/ppermute | solution.py:41
  59.8 3.5 %collective-permute-done.4 = s32[128,8]{1,0:T(8,128)S(1)} collective-permute-done((s32[128,8]{1,0:T(8,128)S(1)}, s32[128,8]{1,0:T(8,128)S(1)}, u32[]{:S(2)}, u32[]{:S(2)}) %collective-permute-start.4) | collective-permute-done | bytes 4128 | tf_op jit(solution)/shard_map/ppermute | solution.py:41
  63.8 0.4 select_reduce_fusion.4
  64.2 0.4 select_reduce_fusion.3
  64.6 0.6 select_reduce_fusion.2
  65.4 0.2 select_reduce_fusion.6
  65.7 0.7 select_reduce_fusion.1
  66.3 1.9 fusion.2
  68.3 61.6 %all-to-all-done.1 = bf16[256,8,1024]{2,1,0:T(8,128)(2,1)} async-done(((bf16[256,8,1024]{2,1,0:T(8,128)(2,1)}), bf16[256,8,1024]{2,1,0:T(8,128)(2,1)}, u32[]{:S(2)}, u32[]{:S(2)}) %all-to-all-start.1) | async-done | bytes 4194336 | tf_op jit(solution)/shard_map/all_to_all | solution.py:133
  129.8 6.1 %convolution_convert_fusion.1 = bf16[512,1024]{1,0:T(8,128)(2,1)} fusion(bf16[512,2048]{1,0:T(8,128)(2,1)} %fusion.2, bf16[2048,1024]{1,0:T(8,128)(2,1)} %bitcast.32), kind=kOutput, calls=%fused_computation.29 | convolution fusion | flops 2148007936 | bytes 7340032 | tf_op jit(solution)/shard_map/dot_general | solution.py:32
  136.1 1.3 pad_maximum_fusion
  137.4 1.3 all_to_all.33
  138.7 8.0 %all-to-all-start.2 = ((bf16[256,2,1152]{2,1,0:T(2,128)(2,1)}), bf16[256,2,1152]{2,1,0:T(2,128)(2,1)}, u32[]{:S(2)}, u32[]{:S(2)}) async-start(bf16[256,2,1152]{2,1,0:T(2,128)(2,1)} %all_to_all.33), calls=%async_computation.2 | async-start | bytes 2359296 | tf_op jit(solution)/shard_map/all_to_all | solution.py:164
  146.9 2.0 convolution_convert_fusion
  148.9 0.2 collective-permute-start.6
  149.1 0.4 collective-permute-start.5
  149.5 0.4 copy-done.2
  149.9 0.2 fusion.12.pick_ref
  150.1 1.5 collective-permute-done.6
  151.7 1.0 copy-done.3
  152.7 0.8 collective-permute-done.5
  153.5 6.0 %fusion.8.terms_ref = f32[512,1024]{1,0:T(8,128)} fusion(bf16[512,1024]{1,0:T(8,128)(2,1)} %copy-done.3, bf16[512,1024]{1,0:T(8,128)(2,1)} %copy-done.2, bf16[512,1024]{1,0:T(8,128)(2,1)} %collective-permute-done.5, bf16[512,1024]{1,0:T(8,128)(2,1)} %convolution_convert_fusion.1, s32[512]{0:T(512)S(1)} %fusion.57), kind=kOutput, calls=%fused_computation.18 | convolution fusion | flops 2156920832 | bytes 6293504 | tf_op jit(solution)/shard_map/dot_general | solution.py:36
  159.5 21.1 %all-to-all-done.2 = bf16[256,2,1152]{2,1,0:T(2,128)(2,1)} async-done(((bf16[256,2,1152]{2,1,0:T(2,128)(2,1)}), bf16[256,2,1152]{2,1,0:T(2,128)(2,1)}, u32[]{:S(2)}, u32[]{:S(2)}) %all-to-all-start.2) | async-done | bytes 1179680 | tf_op jit(solution)/shard_map/all_to_all | solution.py:164
  180.6 3.7 %all_to_all.35 = bf16[512,1152]{1,0:T(8,128)(2,1)} reshape(bf16[256,2,1152]{2,1,0:T(2,128)(2,1)} %all-to-all-done.2) | data formatting | bytes 2359296 | tf_op jit(solution)/shard_map/all_to_all | solution.py:164
  184.3 1.8 fusion.69
  186.3 1.9 collective-permute-done.7.other_ref
  188.2 2.5 %shard_map.37 = bf16[4,4,128,256]{3,2,1,0:T(8,128)(2,1)S(1)} custom-call(bf16[256,1024]{1,0:T(8,128)(2,1)S(1)} %pad_maximum_fusion.1.own_ref, bf16[256,1024]{1,0:T(8,128)(2,1)S(1)} %collective-permute-done.7.other_ref, bf16[512,1024]{1,0:T(8,128)(2,1)S(1)} %fusion.12.pick_ref, f32[512,1024]{1,0:T(8,128)S(1)} %copy-done.1), custom_call_target="tpu_custom_call" | custom-call | flops 1342177280 | bytes 6291456 | tf_op jit(solution)/shard_map/pallas_call | solution.py:88
  190.8 20.6 %all_to_all.43 = bf16[16,128,256]{2,1,0:T(8,128)(2,1)S(1)} all-to-all(bf16[16,128,256]{2,1,0:T(8,128)(2,1)S(1)} %bitcast.70), channel_id=1, replica_groups=mesh['x'=4,'z'=8,'core'=2,'group'=4] {'x','group'}, dimensions={0} | all-to-all | bytes 2097152 | tf_op jit(solution)/shard_map/all_to_all | solution.py:197
  211.5 11.5 %all_to_all.44 = f32[8,16,256]{2,1,0:T(8,128)S(1)} all-to-all(f32[8,16,256]{2,1,0:T(8,128)S(1)} %convert_add_fusion), channel_id=1, replica_groups=mesh['x'=4,'z'=8,'core'=2,'group'=4] {'z'}, dimensions={0} | all-to-all | bytes 262144 | tf_op jit(solution)/shard_map/all_to_all | solution.py:200
  223.0 0.6 fusion.43
  (58 shorter events, 2.5 us)
Async XLA Ops:
  0.0 11.1 %copy-start = (bf16[1024,1024]{1,0:T(8,128)(2,1)S(1)}, bf16[1024,1024]{1,0:T(8,128)(2,1)}, u32[]{:S(2)}) copy-start(bf16[1024,1024]{1,0:T(8,128)(2,1)} %param.3) | copy-start | bytes 6291460
  2.6 16.5 %all-to-all-start = ((s32[8,1,1024]{2,1,0:T(1,128)}), s32[8,1,1024]{2,1,0:T(1,128)S(1)}, u32[]{:S(2)}, u32[]{:S(2)}) async-start(s32[8,1,1024]{2,1,0:T(1,128)} %broadcast_in_dim.93), calls=%async_computation | async-start | bytes 65536 | tf_op jit(solution)/shard_map/all_to_all | solution.py:125
  19.1 110.7 %all-to-all-start.1 = ((bf16[256,8,1024]{2,1,0:T(8,128)(2,1)}), bf16[256,8,1024]{2,1,0:T(8,128)(2,1)}, u32[]{:S(2)}, u32[]{:S(2)}) async-start(bf16[256,8,1024]{2,1,0:T(8,128)(2,1)} %bitcast.71), calls=%async_computation.1 | async-start | bytes 8388608 | tf_op jit(solution)/shard_map/all_to_all | solution.py:133
  40.5 5.2 %collective-permute-start = (s32[8,128]{1,0:T(8,128)S(1)}, s32[8,128]{1,0:T(8,128)S(1)}, u32[]{:S(2)}, u32[]{:S(2)}) collective-permute-start(s32[8,128]{1,0:T(8,128)S(1)} %select_bitcast_fusion.12), channel_id=1, source_target_pairs={{0,128},{64,192},{128,0},{192,64},{1,129},{65,193},{129,1},{193,65... | collective-permute-start | bytes 12296 | tf_op jit(solution)/shard_map/ppermute | solution.py:41
  45.8 3.7 %collective-permute-start.1 = (s32[16,64]{1,0:T(8,128)S(1)}, s32[16,64]{1,0:T(8,128)S(1)}, u32[]{:S(2)}, u32[]{:S(2)}) collective-permute-start(s32[16,64]{1,0:T(8,128)S(1)} %select_bitcast_fusion.11), channel_id=1, source_target_pairs={{0,64},{64,0},{128,192},{192,128},{1,65},{65,1},{129,193},{193,129... | collective-permute-start | bytes 12296 | tf_op jit(solution)/shard_map/ppermute | solution.py:41
  49.8 1.3 collective-permute-start.2
  51.3 5.7 %collective-permute-start.3 = (s32[64,16]{1,0:T(8,128)S(1)}, s32[64,16]{1,0:T(8,128)S(1)}, u32[]{:S(2)}, u32[]{:S(2)}) collective-permute-start(s32[64,16]{1,0:T(8,128)S(1)} %select_bitcast_fusion.5), channel_id=1, source_target_pairs={{0,2},{1,3},{2,0},{3,1},{4,6},{5,7},{6,4},{7,5},{8,10},{9,11},{10,... | collective-permute-start | bytes 12296 | tf_op jit(solution)/shard_map/ppermute | solution.py:41
  57.4 6.0 %collective-permute-start.4 = (s32[128,8]{1,0:T(8,128)S(1)}, s32[128,8]{1,0:T(8,128)S(1)}, u32[]{:S(2)}, u32[]{:S(2)}) collective-permute-start(s32[128,8]{1,0:T(8,128)S(1)} %select_bitcast_fusion.2), channel_id=1, source_target_pairs={{0,1},{1,0},{2,3},{3,2},{4,5},{5,4},{6,7},{7,6},{8,9},{9,8},{10,11... | collective-permute-start | bytes 12296 | tf_op jit(solution)/shard_map/ppermute | solution.py:41
  138.7 41.9 %all-to-all-start.2 = ((bf16[256,2,1152]{2,1,0:T(2,128)(2,1)}), bf16[256,2,1152]{2,1,0:T(2,128)(2,1)}, u32[]{:S(2)}, u32[]{:S(2)}) async-start(bf16[256,2,1152]{2,1,0:T(2,128)(2,1)} %all_to_all.33), calls=%async_computation.2 | async-start | bytes 2359296 | tf_op jit(solution)/shard_map/all_to_all | solution.py:164
  148.9 1.0 copy-start.2
  148.9 2.7 %collective-permute-start.6 = (bf16[512,1024]{1,0:T(8,128)(2,1)S(1)}, bf16[512,1024]{1,0:T(8,128)(2,1)S(1)}, u32[]{:S(2)}, u32[]{:S(2)}) collective-permute-start(bf16[512,1024]{1,0:T(8,128)(2,1)S(1)} %convolution_convert_fusion), channel_id=1, source_target_pairs={{0,4},{4,0},{1,5},{5,1},{2,6},{6,2},{3,7},{7,3},{8,12},{12,8},{9,1... | collective-permute-start | bytes 3145736 | tf_op jit(solution)/shard_map/ppermute | solution.py:41
  149.1 4.4 %collective-permute-start.5 = (bf16[512,1024]{1,0:T(8,128)(2,1)}, bf16[512,1024]{1,0:T(8,128)(2,1)}, u32[]{:S(2)}, u32[]{:S(2)}) collective-permute-start(bf16[512,1024]{1,0:T(8,128)(2,1)} %convolution_convert_fusion.1), channel_id=1, source_target_pairs={{0,4},{4,0},{1,5},{5,1},{2,6},{6,2},{3,7},{7,3},{8,12},{12,8},{9,1... | collective-permute-start | bytes 3145736 | tf_op jit(solution)/shard_map/ppermute | solution.py:41
  151.7 1.0 copy-start.3
  184.3 3.9 %copy-start.1 = (f32[512,1024]{1,0:T(8,128)S(1)}, f32[512,1024]{1,0:T(8,128)}, u32[]{:S(2)}) copy-start(f32[512,1024]{1,0:T(8,128)} %fusion.8.terms_ref) | copy-start | bytes 6291460
  186.2 2.0 collective-permute-start.7

commit v5 on v4

--- a/solution.py
+++ b/solution.py
@@ -59,6 +59,90 @@
     return held.reshape(shape)
 
 
+def pack_rows(targets, rows, slots):
+    count, width = rows.shape
+    step = 256
+
+    def kernel(targets_ref, rows_ref, out_ref):
+        first = pl.program_id(0) * step
+        names = lax.broadcasted_iota(jnp.int32, (step, count), 0) + first
+        hits = (names == targets_ref[...]).astype(jnp.float32).astype(jnp.bfloat16)
+        out_ref[...] = dot(hits, rows_ref[...]).astype(jnp.bfloat16)
+
+    return pl.pallas_call(
+        kernel,
+        grid=(slots // step,),
+        in_specs=[
+            pl.BlockSpec((1, count), lambda i: (0, 0)),
+            pl.BlockSpec((count, width), lambda i: (0, 0)),
+        ],
+        out_specs=pl.BlockSpec((step, width), lambda i: (i, 0)),
+        out_shape=jax.ShapeDtypeStruct((slots, width), jnp.bfloat16),
+        compiler_params=pltpu.CompilerParams(vmem_limit_bytes=60 * 1024 * 1024),
+        cost_estimate=pl.CostEstimate(
+            flops=2 * slots * count * width, bytes_accessed=6 * 1024 * 1024, transcendentals=0
+        ),
+    )(targets[None, :], rows)
+
+
+def slot_sums(slots_of, rows, tail):
+    count, width = rows.shape
+    slots, lanes = tail.shape
+    step = 256
+
+    def kernel(slots_ref, rows_ref, tail_ref, out_ref, hits_ref):
+        j = pl.program_id(0)
+
+        @pl.when(j == 0)
+        def _():
+            names = lax.broadcasted_iota(jnp.int32, (slots, step), 0)
+            for at in range(0, count, step):
+                hits = names == slots_ref[:, at : at + step]
+                hits_ref[:, at : at + step] = hits.astype(jnp.float32).astype(jnp.bfloat16)
+            out_ref[:, width:] = tail_ref[...]
+
+        here = pl.ds(pl.multiple_of(j * step, step), step)
+        out_ref[:, here] = dot(hits_ref[...], rows_ref[...]).astype(jnp.bfloat16)
+
+    return pl.pallas_call(
+        kernel,
+        grid=(width // step,),
+        in_specs=[
+            pl.BlockSpec((1, count), lambda j: (0, 0)),
+            pl.BlockSpec((count, step), lambda j: (0, j)),
+            pl.BlockSpec((slots, lanes), lambda j: (0, 0)),
+        ],
+        out_specs=pl.BlockSpec((slots, width + lanes), lambda j: (0, 0)),
+        out_shape=jax.ShapeDtypeStruct((slots, width + lanes), jnp.bfloat16),
+        scratch_shapes=[pltpu.VMEM((slots, count), jnp.bfloat16)],
+        compiler_params=pltpu.CompilerParams(vmem_limit_bytes=16 * 1024 * 1024),
+        cost_estimate=pl.CostEstimate(
+            flops=2 * slots * count * width, bytes_accessed=6 * 1024 * 1024, transcendentals=0
+        ),
+    )(slots_of[None, :], rows, tail)
+
+
+def firm_halves(came, firms, width):
+    count, lanes = came.shape[0], came.shape[1] - width
+
+    def kernel(came_ref, out_ref):
+        names = lax.broadcasted_iota(jnp.int32, (count, lanes), 1).astype(jnp.float32)
+        hits = (came_ref[:, width:].astype(jnp.float32) == names).astype(jnp.float32).astype(jnp.bfloat16)
+        sums = gram(hits, came_ref[:, :width])
+        high = sums.astype(jnp.bfloat16)
+        out_ref[:firms] = high
+        out_ref[firms:] = (sums - high.astype(jnp.float32)).astype(jnp.bfloat16)
+
+    return pl.pallas_call(
+        kernel,
+        out_shape=jax.ShapeDtypeStruct((2 * firms, width), jnp.bfloat16),
+        compiler_params=pltpu.CompilerParams(vmem_limit_bytes=12 * 1024 * 1024),
+        cost_estimate=pl.CostEstimate(
+            flops=2 * count * firms * width, bytes_accessed=2 * 1024 * 1024, transcendentals=0
+        ),
+    )(came)
+
+
 def all_terms(own, other, pick, worker_terms, row_parts, col_parts):
     firms, width = own.shape[0] // 2, own.shape[1]
     picked = pick.shape[0]
@@ -101,7 +185,7 @@
             pltpu.VMEM((2 * firms, width), jnp.bfloat16),
             pltpu.VMEM((picked, 4 * firms), jnp.bfloat16),
         ],
-        compiler_params=pltpu.CompilerParams(vmem_limit_bytes=24 * 1024 * 1024),
+        compiler_params=pltpu.CompilerParams(vmem_limit_bytes=12 * 1024 * 1024),
         cost_estimate=pl.CostEstimate(
             flops=2 * picked * width * 10 * firms, bytes_accessed=6 * 1024 * 1024, transcendentals=0
         ),
@@ -128,7 +212,7 @@
 
         home = worker_ids % classes
         target = home * capacity + equal_before(home)
-        packed = dot(one_hot(target, classes * capacity), scores).astype(jnp.bfloat16)
+        packed = pack_rows(target, scores, classes * capacity)
         packed, raw = lax.optimization_barrier((packed, raw))
         got = lax.all_to_all(packed, EVERYONE, 0, 0, tiled=True)
 
@@ -158,12 +242,11 @@
         row_slot = jnp.max(jnp.where(pair_rows == pair[None, :], pair_slot[:, None], -1), axis=0)
         sent_firm = placed_values(pair_slot, pair_firm // classes, 2 * classes)
 
-        to_slots, got = lax.optimization_barrier((one_hot(row_slot, 2 * classes), got))
-        sent = dot(to_slots, got).astype(jnp.bfloat16)
         tail = jnp.broadcast_to(sent_firm.astype(jnp.bfloat16)[:, None], (2 * classes, LANES))
-        came = lax.all_to_all(
-            jnp.concatenate([sent, tail], axis=1), EVERYONE, 0, 0, tiled=True
-        )
+        tail, row_slot, got = lax.optimization_barrier((tail, row_slot, got))
+        sent = slot_sums(row_slot, got, tail)
+        came = lax.all_to_all(sent, EVERYONE, 0, 0, tiled=True)
+        sent = sent[:, :width]
 
         half = workers_here
         other_slot = jnp.concatenate([pair_slot[half:], pair_slot[:half]])
@@ -184,12 +267,7 @@
         worker_terms = gram(left, right)
 
         came, worker_terms, pick = lax.optimization_barrier((came, worker_terms, pick))
-        firm_names = jnp.arange(firms_here, dtype=jnp.float32).astype(jnp.bfloat16)
-        firm_hits = (came[:, width:] == firm_names[None, :]).astype(jnp.bfloat16)
-        firm_sums = gram(firm_hits, came[:, :width])
-        high = lax.optimization_barrier(firm_sums.astype(jnp.bfloat16))
-        low = (firm_sums - high.astype(jnp.float32)).astype(jnp.bfloat16)
-        firm_pair = jnp.concatenate([high, low], axis=0)
+        firm_pair = firm_halves(came, firms_here, width)
         terms = all_terms(
             firm_pair, swapped(firm_pair, "core", 1), pick, worker_terms, x_count, group_count
         )

time: 224 us -> 221 us (0.987)
  matrix products: 21.9 us -> 6.47 us
  Pallas kernels: 2.54 us -> 16.4 us
  other arithmetic: 18.4 us -> 15.5 us
    pallas_call x0 -> x3, Pallas kernels: none -> 13.8 us  [the longest x1 8.39 us: pack_rows(): pl.pallas_call(kernel, grid=(slots // step,), in_specs=[pl.BlockSpec((1,...]
    dot_general x3 -> x1, matrix products: 14.1 us -> 0.77 us  [dot(): return jnp.dot(a, b, preferred_element_type=jnp.float32)]
    all_to_all x2, local copies, waits for them, and re-layouts: 4.99 us -> 1.76 us  [local(): came = lax.all_to_all(sent, EVERYONE, 0, 0, tiled=True)]
    all_to_all x1, waiting for transfers between devices: 21.1 us -> 23.5 us  [local(): came = lax.all_to_all(sent, EVERYONE, 0, 0, tiled=True)]
    dot_general x2 -> x1, matrix products: 7.8 us -> 5.7 us  [gram(): lax.dot_general(a, b, (((0,), (0,)), ((), ())), preferred_element_type=jn...]
  transfers between devices with their start and end apart: 11 -> 11, of which waited for: 11 -> 10; matrix products, arithmetic and copies ran while one was open for 13% -> 9% of each run, Pallas kernels for 0% -> 4%
where the time goes in v5:
time: 221 us; the launch traced here: 220 us
  waiting for transfers between devices  104 us (47%)
  starting transfers between devices  39.3 us (18%)
  blocking collectives  32 us (14%)
  Pallas kernels  16.4 us (7%)
  other arithmetic  15.5 us (7%)
  local copies, waits for them, and re-layouts  6.52 us (3%)
  matrix products  6.47 us (3%)
    all_to_all x1, waiting for transfers between devices, local(): got = lax.all_to_all(packed, EVERYONE, 0, 0, tiled=True)  63.5 us
    all_to_all x1, waiting for transfers between devices, local(): came = lax.all_to_all(sent, EVERYONE, 0, 0, tiled=True)  23.5 us
    all_to_all x1, blocking collectives, local(): terms = lax.all_to_all(terms, ('x', 'group'), 0, 0, tiled=True)  20.6 us
    ppermute x8, waiting for transfers between devices, swapped(): return lax.ppermute(value, axis, [(i, i ^ bit) for i in range(size)])  16.7 us
    all_to_all x1, starting transfers between devices, local(): got = lax.all_to_all(packed, EVERYONE, 0, 0, tiled=True)  14.3 us
    all_to_all x1, blocking collectives, local(): lax.all_to_all(terms.reshape(z_count, block_rows, block_cols), 'z', 0, 0,...  11.5 us
    ppermute x8, starting transfers between devices, swapped(): return lax.ppermute(value, axis, [(i, i ^ bit) for i in range(size)])  10 us
    all_to_all x1, starting transfers between devices, local(): lax.all_to_all(jnp.broadcast_to(raw[None, :], (z_count, local_rows)), 'z'...  8.47 us
  transfers between devices with their start and end apart: 11, of which 10 were waited for; matrix products, arithmetic and copies ran while one was open for 9% of the time, Pallas kernels for 4%

profile of v5, /device:TPU:8, one launch (start us, length us, event | category | flops | bytes accessed | tf_op | source)
XLA Modules:
  0.0 220.2 jit_solution(15363065840546541589)
XLA Ops:
  0.0 0.7 add_select_fusion.12
  0.7 0.4 convert_reduce_fusion.1
  1.1 1.3 multiply_add_fusion
  2.4 0.6 broadcast_in_dim.140
  3.1 8.5 %all-to-all-start = ((s32[8,1,1024]{2,1,0:T(1,128)}), s32[8,1,1024]{2,1,0:T(1,128)S(1)}, u32[]{:S(2)}, u32[]{:S(2)}) async-start(s32[8,1,1024]{2,1,0:T(1,128)} %broadcast_in_dim.140), calls=%async_computation | async-start | bytes 65536 | tf_op jit(solution)/shard_map/all_to_all | solution.py:209
  11.5 8.4 %shard_map.37 = bf16[2048,1024]{1,0:T(8,128)(2,1)} custom-call(s32[1,1024]{1,0:T(1,128)} %bitcast.92, bf16[1024,1024]{1,0:T(8,128)(2,1)} %rows_ref.1), custom_call_target="tpu_custom_call" | custom-call | flops 4294967296 | bytes 6291456 | tf_op jit(solution)/shard_map/pallas_call | solution.py:72
  19.9 14.3 %all-to-all-start.1 = ((bf16[256,8,1024]{2,1,0:T(8,128)(2,1)}), bf16[256,8,1024]{2,1,0:T(8,128)(2,1)}, u32[]{:S(2)}, u32[]{:S(2)}) async-start(bf16[256,8,1024]{2,1,0:T(8,128)(2,1)} %bitcast.70), calls=%async_computation.1 | async-start | bytes 8388608 | tf_op jit(solution)/shard_map/all_to_all | solution.py:217
  34.3 0.3 iota_compare_fusion.1
  34.7 7.2 %convert_reduce_fusion = s32[8,1024]{1,0:T(8,128)S(1)} fusion(s32[8,1024]{1,0:T(8,128)S(1)} %fusion.22, pred[1024,1024]{1,0:T(8,128)(4,1)S(1)} %iota_compare_fusion.1), kind=kLoop, calls=%fused_computation | loop fusion | flops 33546240 | bytes 1114112 | tf_op jit(solution)/shard_map/vmap()/reduce_sum | solution.py:18
  42.0 1.2 select_reduce_fusion
  43.3 3.1 %collective-permute-start = (s32[8,128]{1,0:T(8,128)S(1)}, s32[8,128]{1,0:T(8,128)S(1)}, u32[]{:S(2)}, u32[]{:S(2)}) collective-permute-start(s32[8,128]{1,0:T(8,128)S(1)} %select_bitcast_fusion.12), channel_id=1, source_target_pairs={{0,128},{64,192},{128,0},{192,64},{1,129},{65,193},{129,1},{193,65... | collective-permute-start | bytes 12296 | tf_op jit(solution)/shard_map/ppermute | solution.py:41
  46.3 2.2 collective-permute-done
  48.6 1.5 collective-permute-start.1
  50.2 2.2 %collective-permute-done.1 = s32[16,64]{1,0:T(8,128)S(1)} collective-permute-done((s32[16,64]{1,0:T(8,128)S(1)}, s32[16,64]{1,0:T(8,128)S(1)}, u32[]{:S(2)}, u32[]{:S(2)}) %collective-permute-start.1) | collective-permute-done | bytes 4128 | tf_op jit(solution)/shard_map/ppermute | solution.py:41
  52.7 1.2 collective-permute-done.2
  54.1 2.2 collective-permute-start.3
  56.3 3.5 %collective-permute-done.3 = s32[64,16]{1,0:T(8,128)S(1)} collective-permute-done((s32[64,16]{1,0:T(8,128)S(1)}, s32[64,16]{1,0:T(8,128)S(1)}, u32[]{:S(2)}, u32[]{:S(2)}) %collective-permute-start.3) | collective-permute-done | bytes 4128 | tf_op jit(solution)/shard_map/ppermute | solution.py:41
  60.2 2.5 %collective-permute-start.4 = (s32[128,8]{1,0:T(8,128)S(1)}, s32[128,8]{1,0:T(8,128)S(1)}, u32[]{:S(2)}, u32[]{:S(2)}) collective-permute-start(s32[128,8]{1,0:T(8,128)S(1)} %select_bitcast_fusion.2), channel_id=1, source_target_pairs={{0,1},{1,0},{2,3},{3,2},{4,5},{5,4},{6,7},{7,6},{8,9},{9,8},{10,11... | collective-permute-start | bytes 12296 | tf_op jit(solution)/shard_map/ppermute | solution.py:41
  62.6 3.5 %collective-permute-done.4 = s32[128,8]{1,0:T(8,128)S(1)} collective-permute-done((s32[128,8]{1,0:T(8,128)S(1)}, s32[128,8]{1,0:T(8,128)S(1)}, u32[]{:S(2)}, u32[]{:S(2)}) %collective-permute-start.4) | collective-permute-done | bytes 4128 | tf_op jit(solution)/shard_map/ppermute | solution.py:41
  66.3 0.2 reshape_reshape.3
  66.6 0.4 select_reduce_fusion.4
  67.0 0.4 select_reduce_fusion.3
  67.4 0.6 select_reduce_fusion.2
  68.2 0.2 select_reduce_fusion.6
  68.5 0.7 select_reduce_fusion.1
  69.1 63.5 %all-to-all-done.1 = bf16[256,8,1024]{2,1,0:T(8,128)(2,1)} async-done(((bf16[256,8,1024]{2,1,0:T(8,128)(2,1)}), bf16[256,8,1024]{2,1,0:T(8,128)(2,1)}, u32[]{:S(2)}, u32[]{:S(2)}) %all-to-all-start.1) | async-done | bytes 4194336 | tf_op jit(solution)/shard_map/all_to_all | solution.py:217
  132.8 5.1 %shard_map.38 = bf16[512,1152]{1,0:T(8,128)(2,1)S(1)} custom-call(s32[1,2048]{1,0:T(1,128)S(1)} %bitcast.69, bf16[2048,1024]{1,0:T(8,128)(2,1)} %bitcast.33.rows_ref, bf16[512,128]{1,0:T(8,128)(2,1)S(1)} %broadcast_in_dim.152.tail_ref), custom_call_target="tpu_custom_call" | custom-call | flops 2147483648 | bytes 6291456 | tf_op jit(solution)/shard_map/pallas_call | solution.py:107
  137.9 1.3 all_to_all.33
  139.2 6.5 %all-to-all-start.2 = ((bf16[256,2,1152]{2,1,0:T(2,128)(2,1)}), bf16[256,2,1152]{2,1,0:T(2,128)(2,1)S(1)}, u32[]{:S(2)}, u32[]{:S(2)}) async-start(bf16[256,2,1152]{2,1,0:T(2,128)(2,1)} %all_to_all.33), calls=%async_computation.2 | async-start | bytes 2359296 | tf_op jit(solution)/shard_map/all_to_all | solution.py:248
  145.7 0.2 select_reduce_fusion.5
  146.1 0.8 convolution_convert_fusion
  146.9 0.2 collective-permute-start.6
  147.1 0.4 collective-permute-start.5
  147.5 0.4 copy-done.1
  147.8 0.2 fusion.8.pick_ref
  148.1 1.6 collective-permute-done.6
  149.6 1.0 copy-done.2
  150.6 0.6 collective-permute-done.5
  151.2 5.7 %fusion.4.terms_ref = f32[512,1024]{1,0:T(8,128)} fusion(bf16[512,1024]{1,0:T(8,128)(2,1)} %copy-done.2, bf16[512,1024]{1,0:T(8,128)(2,1)} %copy-done.1, bf16[512,1024]{1,0:T(8,128)(2,1)} %collective-permute-done.5, bf16[512,1024]{1,0:T(8,128)(2,1)S(1)} %slice.168, s32[512]{0:T(512)S(1)} %fusion.48), kind=kOutput, calls=%fused_computation.12 | convolution fusion | flops 2156920832 | bytes 6293504 | tf_op jit(solution)/shard_map/dot_general | solution.py:36
  156.9 23.5 %all-to-all-done.2 = bf16[256,2,1152]{2,1,0:T(2,128)(2,1)S(1)} async-done(((bf16[256,2,1152]{2,1,0:T(2,128)(2,1)}), bf16[256,2,1152]{2,1,0:T(2,128)(2,1)S(1)}, u32[]{:S(2)}, u32[]{:S(2)}) %all-to-all-start.2) | async-done | bytes 1179680 | tf_op jit(solution)/shard_map/all_to_all | solution.py:248
  180.4 0.5 all_to_all.35.came_ref
  180.9 0.3 shard_map.39.own_ref
  181.3 1.9 collective-permute-done.7.other_ref
  183.2 1.6 copy-done
  184.8 2.5 %shard_map.40 = bf16[4,4,128,256]{3,2,1,0:T(8,128)(2,1)S(1)} custom-call(bf16[256,1024]{1,0:T(8,128)(2,1)S(1)} %shard_map.39.own_ref, bf16[256,1024]{1,0:T(8,128)(2,1)S(1)} %collective-permute-done.7.other_ref, bf16[512,1024]{1,0:T(8,128)(2,1)S(1)} %fusion.8.pick_ref, f32[512,1024]{1,0:T(8,128)S(1)} %copy-done), custom_call_target="tpu_custom_call" | custom-call | flops 1342177280 | bytes 6291456 | tf_op jit(solution)/shard_map/pallas_call | solution.py:172
  187.4 20.6 %all_to_all.43 = bf16[16,128,256]{2,1,0:T(8,128)(2,1)S(1)} all-to-all(bf16[16,128,256]{2,1,0:T(8,128)(2,1)S(1)} %bitcast.68), channel_id=1, replica_groups=mesh['x'=4,'z'=8,'core'=2,'group'=4] {'x','group'}, dimensions={0} | all-to-all | bytes 2097152 | tf_op jit(solution)/shard_map/all_to_all | solution.py:275
  208.1 11.5 %all_to_all.44 = f32[8,16,256]{2,1,0:T(8,128)S(1)} all-to-all(f32[8,16,256]{2,1,0:T(8,128)S(1)} %convert_add_fusion), channel_id=1, replica_groups=mesh['x'=4,'z'=8,'core'=2,'group'=4] {'z'}, dimensions={0} | all-to-all | bytes 262144 | tf_op jit(solution)/shard_map/all_to_all | solution.py:278
  219.6 0.6 fusion.34
  (52 shorter events, 2.2 us)
Async XLA Ops:
  3.1 16.9 %all-to-all-start = ((s32[8,1,1024]{2,1,0:T(1,128)}), s32[8,1,1024]{2,1,0:T(1,128)S(1)}, u32[]{:S(2)}, u32[]{:S(2)}) async-start(s32[8,1,1024]{2,1,0:T(1,128)} %broadcast_in_dim.140), calls=%async_computation | async-start | bytes 65536 | tf_op jit(solution)/shard_map/all_to_all | solution.py:209
  19.9 112.7 %all-to-all-start.1 = ((bf16[256,8,1024]{2,1,0:T(8,128)(2,1)}), bf16[256,8,1024]{2,1,0:T(8,128)(2,1)}, u32[]{:S(2)}, u32[]{:S(2)}) async-start(bf16[256,8,1024]{2,1,0:T(8,128)(2,1)} %bitcast.70), calls=%async_computation.1 | async-start | bytes 8388608 | tf_op jit(solution)/shard_map/all_to_all | solution.py:217
  43.3 5.2 %collective-permute-start = (s32[8,128]{1,0:T(8,128)S(1)}, s32[8,128]{1,0:T(8,128)S(1)}, u32[]{:S(2)}, u32[]{:S(2)}) collective-permute-start(s32[8,128]{1,0:T(8,128)S(1)} %select_bitcast_fusion.12), channel_id=1, source_target_pairs={{0,128},{64,192},{128,0},{192,64},{1,129},{65,193},{129,1},{193,65... | collective-permute-start | bytes 12296 | tf_op jit(solution)/shard_map/ppermute | solution.py:41
  48.6 3.7 %collective-permute-start.1 = (s32[16,64]{1,0:T(8,128)S(1)}, s32[16,64]{1,0:T(8,128)S(1)}, u32[]{:S(2)}, u32[]{:S(2)}) collective-permute-start(s32[16,64]{1,0:T(8,128)S(1)} %select_bitcast_fusion.11), channel_id=1, source_target_pairs={{0,64},{64,0},{128,192},{192,128},{1,65},{65,1},{129,193},{193,129... | collective-permute-start | bytes 12296 | tf_op jit(solution)/shard_map/ppermute | solution.py:41
  52.6 1.3 collective-permute-start.2
  54.1 5.7 %collective-permute-start.3 = (s32[64,16]{1,0:T(8,128)S(1)}, s32[64,16]{1,0:T(8,128)S(1)}, u32[]{:S(2)}, u32[]{:S(2)}) collective-permute-start(s32[64,16]{1,0:T(8,128)S(1)} %select_bitcast_fusion.5), channel_id=1, source_target_pairs={{0,2},{1,3},{2,0},{3,1},{4,6},{5,7},{6,4},{7,5},{8,10},{9,11},{10,... | collective-permute-start | bytes 12296 | tf_op jit(solution)/shard_map/ppermute | solution.py:41
  60.2 6.0 %collective-permute-start.4 = (s32[128,8]{1,0:T(8,128)S(1)}, s32[128,8]{1,0:T(8,128)S(1)}, u32[]{:S(2)}, u32[]{:S(2)}) collective-permute-start(s32[128,8]{1,0:T(8,128)S(1)} %select_bitcast_fusion.2), channel_id=1, source_target_pairs={{0,1},{1,0},{2,3},{3,2},{4,5},{5,4},{6,7},{7,6},{8,9},{9,8},{10,11... | collective-permute-start | bytes 12296 | tf_op jit(solution)/shard_map/ppermute | solution.py:41
  139.2 41.2 %all-to-all-start.2 = ((bf16[256,2,1152]{2,1,0:T(2,128)(2,1)}), bf16[256,2,1152]{2,1,0:T(2,128)(2,1)S(1)}, u32[]{:S(2)}, u32[]{:S(2)}) async-start(bf16[256,2,1152]{2,1,0:T(2,128)(2,1)} %all_to_all.33), calls=%async_computation.2 | async-start | bytes 2359296 | tf_op jit(solution)/shard_map/all_to_all | solution.py:248
  146.8 1.0 copy-start.1
  146.9 2.8 %collective-permute-start.6 = (bf16[512,1024]{1,0:T(8,128)(2,1)S(1)}, bf16[512,1024]{1,0:T(8,128)(2,1)S(1)}, u32[]{:S(2)}, u32[]{:S(2)}) collective-permute-start(bf16[512,1024]{1,0:T(8,128)(2,1)S(1)} %convolution_convert_fusion), channel_id=1, source_target_pairs={{0,4},{4,0},{1,5},{5,1},{2,6},{6,2},{3,7},{7,3},{8,12},{12,8},{9,1... | collective-permute-start | bytes 3145736 | tf_op jit(solution)/shard_map/ppermute | solution.py:41
  147.1 4.1 %collective-permute-start.5 = (bf16[512,1024]{1,0:T(8,128)(2,1)S(1)}, bf16[512,1024]{1,0:T(8,128)(2,1)}, u32[]{:S(2)}, u32[]{:S(2)}) collective-permute-start(bf16[512,1024]{1,0:T(8,128)(2,1)S(1)} %slice.168), channel_id=1, source_target_pairs={{0,4},{4,0},{1,5},{5,1},{2,6},{6,2},{3,7},{7,3},{8,12},{12,8},{9,1... | collective-permute-start | bytes 3145736 | tf_op jit(solution)/shard_map/ppermute | solution.py:41
  149.6 1.0 copy-start.2
  181.2 2.0 collective-permute-start.7
  183.2 1.6 copy-start

commit v6 on v5

--- a/solution.py
+++ b/solution.py
@@ -61,7 +61,7 @@
 
 def pack_rows(targets, rows, slots):
     count, width = rows.shape
-    step = 256
+    step = 512
 
     def kernel(targets_ref, rows_ref, out_ref):
         first = pl.program_id(0) * step
@@ -88,7 +88,7 @@
 def slot_sums(slots_of, rows, tail):
     count, width = rows.shape
     slots, lanes = tail.shape
-    step = 256
+    step = 512
 
     def kernel(slots_ref, rows_ref, tail_ref, out_ref, hits_ref):
         j = pl.program_id(0)
@@ -205,10 +205,9 @@
         capacity = 2 * local_rows // classes
         core = lax.axis_index("core")
 
-        raw = worker_ids * FIRMS + firm_ids
-        raw = lax.all_to_all(
-            jnp.broadcast_to(raw[None, :], (z_count, local_rows)), "z", 0, 0, tiled=True
-        )
+        raw = jnp.broadcast_to((worker_ids * FIRMS + firm_ids)[None, :], (z_count, local_rows))
+        raw, worker_ids = lax.optimization_barrier((raw, worker_ids))
+        raw = lax.all_to_all(raw, "z", 0, 0, tiled=True)
 
         home = worker_ids % classes
         target = home * capacity + equal_before(home)

time: 221 us -> 220 us (level)
  transfers between devices with their start and end apart: 11 -> 11, of which waited for: 10 -> 10; matrix products, arithmetic and copies ran while one was open for 9% -> 10% of each run, Pallas kernels for 4% -> 3%
where the time goes in v6:
time: 220 us
  waiting for transfers between devices  104 us (47%)
  starting transfers between devices  39.3 us (18%)
  blocking collectives  32 us (15%)
  other arithmetic  16.1 us (7%)
  Pallas kernels  15 us (7%)
  local copies, waits for them, and re-layouts  6.54 us (3%)
  matrix products  6.48 us (3%)
    all_to_all x1, waiting for transfers between devices, local(): got = lax.all_to_all(packed, EVERYONE, 0, 0, tiled=True)  63.5 us
    all_to_all x1, waiting for transfers between devices, local(): came = lax.all_to_all(sent, EVERYONE, 0, 0, tiled=True)  23.5 us
    all_to_all x1, blocking collectives, local(): terms = lax.all_to_all(terms, ('x', 'group'), 0, 0, tiled=True)  20.6 us
    ppermute x8, waiting for transfers between devices, swapped(): return lax.ppermute(value, axis, [(i, i ^ bit) for i in range(size)])  16.7 us
    all_to_all x1, starting transfers between devices, local(): got = lax.all_to_all(packed, EVERYONE, 0, 0, tiled=True)  14.4 us
    all_to_all x1, blocking collectives, local(): lax.all_to_all(terms.reshape(z_count, block_rows, block_cols), 'z', 0, 0,...  11.5 us
    ppermute x8, starting transfers between devices, swapped(): return lax.ppermute(value, axis, [(i, i ^ bit) for i in range(size)])  10 us
    all_to_all x1, starting transfers between devices, local(): raw = lax.all_to_all(raw, 'z', 0, 0, tiled=True)  8.47 us
  transfers between devices with their start and end apart: 11, of which 10 were waited for; matrix products, arithmetic and copies ran while one was open for 10% of the time, Pallas kernels for 3%

profile of v6, /device:TPU:8, one launch (start us, length us, event | category | flops | bytes accessed | tf_op | source)
XLA Modules:
  0.0 219.6 jit_solution(14665753348474041792)
XLA Ops:
  0.0 0.7 multiply_add_fusion.1
  0.7 0.7 all_to_all.30
  1.4 8.5 %all-to-all-start = ((s32[8,1,1024]{2,1,0:T(1,128)}), s32[8,1,1024]{2,1,0:T(1,128)S(1)}, u32[]{:S(2)}, u32[]{:S(2)}) async-start(s32[8,1,1024]{2,1,0:T(1,128)} %all_to_all.30), calls=%async_computation | async-start | bytes 65536 | tf_op jit(solution)/shard_map/all_to_all | solution.py:210
  9.8 0.7 add_select_fusion.12
  10.5 0.4 convert_reduce_fusion.1
  10.9 1.3 multiply_add_fusion
  12.2 7.6 %shard_map.37 = bf16[2048,1024]{1,0:T(8,128)(2,1)} custom-call(s32[1,1024]{1,0:T(1,128)} %bitcast.92, bf16[1024,1024]{1,0:T(8,128)(2,1)} %rows_ref.1), custom_call_target="tpu_custom_call" | custom-call | flops 4294967296 | bytes 6291456 | tf_op jit(solution)/shard_map/pallas_call | solution.py:72
  19.9 14.4 %all-to-all-start.1 = ((bf16[256,8,1024]{2,1,0:T(8,128)(2,1)}), bf16[256,8,1024]{2,1,0:T(8,128)(2,1)}, u32[]{:S(2)}, u32[]{:S(2)}) async-start(bf16[256,8,1024]{2,1,0:T(8,128)(2,1)} %bitcast.70), calls=%async_computation.1 | async-start | bytes 8388608 | tf_op jit(solution)/shard_map/all_to_all | solution.py:216
  34.3 0.3 iota_compare_fusion.1
  34.7 7.2 %convert_reduce_fusion = s32[8,1024]{1,0:T(8,128)S(1)} fusion(s32[8,1024]{1,0:T(8,128)S(1)} %fusion.22, pred[1024,1024]{1,0:T(8,128)(4,1)S(1)} %iota_compare_fusion.1), kind=kLoop, calls=%fused_computation | loop fusion | flops 33546240 | bytes 1114112 | tf_op jit(solution)/shard_map/vmap()/reduce_sum | solution.py:18
  42.0 1.2 select_reduce_fusion
  43.3 3.1 %collective-permute-start = (s32[8,128]{1,0:T(8,128)S(1)}, s32[8,128]{1,0:T(8,128)S(1)}, u32[]{:S(2)}, u32[]{:S(2)}) collective-permute-start(s32[8,128]{1,0:T(8,128)S(1)} %select_bitcast_fusion.12), channel_id=1, source_target_pairs={{0,128},{64,192},{128,0},{192,64},{1,129},{65,193},{129,1},{193,65... | collective-permute-start | bytes 12296 | tf_op jit(solution)/shard_map/ppermute | solution.py:41
  46.3 2.2 collective-permute-done
  48.6 1.5 collective-permute-start.1
  50.2 2.2 %collective-permute-done.1 = s32[16,64]{1,0:T(8,128)S(1)} collective-permute-done((s32[16,64]{1,0:T(8,128)S(1)}, s32[16,64]{1,0:T(8,128)S(1)}, u32[]{:S(2)}, u32[]{:S(2)}) %collective-permute-start.1) | collective-permute-done | bytes 4128 | tf_op jit(solution)/shard_map/ppermute | solution.py:41
  52.7 1.2 collective-permute-done.2
  54.1 2.2 collective-permute-start.3
  56.3 3.5 %collective-permute-done.3 = s32[64,16]{1,0:T(8,128)S(1)} collective-permute-done((s32[64,16]{1,0:T(8,128)S(1)}, s32[64,16]{1,0:T(8,128)S(1)}, u32[]{:S(2)}, u32[]{:S(2)}) %collective-permute-start.3) | collective-permute-done | bytes 4128 | tf_op jit(solution)/shard_map/ppermute | solution.py:41
  60.1 2.5 %collective-permute-start.4 = (s32[128,8]{1,0:T(8,128)S(1)}, s32[128,8]{1,0:T(8,128)S(1)}, u32[]{:S(2)}, u32[]{:S(2)}) collective-permute-start(s32[128,8]{1,0:T(8,128)S(1)} %select_bitcast_fusion.2), channel_id=1, source_target_pairs={{0,1},{1,0},{2,3},{3,2},{4,5},{5,4},{6,7},{7,6},{8,9},{9,8},{10,11... | collective-permute-start | bytes 12296 | tf_op jit(solution)/shard_map/ppermute | solution.py:41
  62.6 3.5 %collective-permute-done.4 = s32[128,8]{1,0:T(8,128)S(1)} collective-permute-done((s32[128,8]{1,0:T(8,128)S(1)}, s32[128,8]{1,0:T(8,128)S(1)}, u32[]{:S(2)}, u32[]{:S(2)}) %collective-permute-start.4) | collective-permute-done | bytes 4128 | tf_op jit(solution)/shard_map/ppermute | solution.py:41
  66.6 0.4 select_reduce_fusion.4
  67.0 0.4 select_reduce_fusion.3
  67.4 0.6 select_reduce_fusion.2
  68.2 0.2 select_reduce_fusion.6
  68.5 0.7 select_reduce_fusion.1
  69.1 63.5 %all-to-all-done.1 = bf16[256,8,1024]{2,1,0:T(8,128)(2,1)} async-done(((bf16[256,8,1024]{2,1,0:T(8,128)(2,1)}), bf16[256,8,1024]{2,1,0:T(8,128)(2,1)}, u32[]{:S(2)}, u32[]{:S(2)}) %all-to-all-start.1) | async-done | bytes 4194336 | tf_op jit(solution)/shard_map/all_to_all | solution.py:216
  132.8 4.5 %shard_map.38 = bf16[512,1152]{1,0:T(8,128)(2,1)S(1)} custom-call(s32[1,2048]{1,0:T(1,128)S(1)} %bitcast.69, bf16[2048,1024]{1,0:T(8,128)(2,1)} %bitcast.33.rows_ref, bf16[512,128]{1,0:T(8,128)(2,1)S(1)} %broadcast_in_dim.152.tail_ref), custom_call_target="tpu_custom_call" | custom-call | flops 2147483648 | bytes 6291456 | tf_op jit(solution)/shard_map/pallas_call | solution.py:107
  137.3 1.3 all_to_all.36
  138.6 6.5 %all-to-all-start.2 = ((bf16[256,2,1152]{2,1,0:T(2,128)(2,1)}), bf16[256,2,1152]{2,1,0:T(2,128)(2,1)S(1)}, u32[]{:S(2)}, u32[]{:S(2)}) async-start(bf16[256,2,1152]{2,1,0:T(2,128)(2,1)} %all_to_all.36), calls=%async_computation.2 | async-start | bytes 2359296 | tf_op jit(solution)/shard_map/all_to_all | solution.py:247
  145.1 0.2 select_reduce_fusion.5
  145.5 0.8 convolution_convert_fusion
  146.3 0.2 collective-permute-start.6
  146.5 0.4 collective-permute-start.5
  146.9 0.4 copy-done.1
  147.2 0.2 fusion.8.pick_ref
  147.5 1.6 collective-permute-done.6
  149.0 1.0 copy-done.2
  150.0 0.6 collective-permute-done.5
  150.6 5.7 %fusion.4.terms_ref = f32[512,1024]{1,0:T(8,128)} fusion(bf16[512,1024]{1,0:T(8,128)(2,1)} %copy-done.2, bf16[512,1024]{1,0:T(8,128)(2,1)} %copy-done.1, bf16[512,1024]{1,0:T(8,128)(2,1)} %collective-permute-done.5, bf16[512,1024]{1,0:T(8,128)(2,1)S(1)} %slice.168, s32[512]{0:T(512)S(1)} %fusion.48), kind=kOutput, calls=%fused_computation.12 | convolution fusion | flops 2156920832 | bytes 6293504 | tf_op jit(solution)/shard_map/dot_general | solution.py:36
  156.3 23.5 %all-to-all-done.2 = bf16[256,2,1152]{2,1,0:T(2,128)(2,1)S(1)} async-done(((bf16[256,2,1152]{2,1,0:T(2,128)(2,1)}), bf16[256,2,1152]{2,1,0:T(2,128)(2,1)S(1)}, u32[]{:S(2)}, u32[]{:S(2)}) %all-to-all-start.2) | async-done | bytes 1179680 | tf_op jit(solution)/shard_map/all_to_all | solution.py:247
  179.8 0.5 all_to_all.38.came_ref
  180.3 0.3 shard_map.39.own_ref
  180.7 1.9 collective-permute-done.7.other_ref
  182.6 1.6 copy-done
  184.2 2.5 %shard_map.40 = bf16[4,4,128,256]{3,2,1,0:T(8,128)(2,1)S(1)} custom-call(bf16[256,1024]{1,0:T(8,128)(2,1)S(1)} %shard_map.39.own_ref, bf16[256,1024]{1,0:T(8,128)(2,1)S(1)} %collective-permute-done.7.other_ref, bf16[512,1024]{1,0:T(8,128)(2,1)S(1)} %fusion.8.pick_ref, f32[512,1024]{1,0:T(8,128)S(1)} %copy-done), custom_call_target="tpu_custom_call" | custom-call | flops 1342177280 | bytes 6291456 | tf_op jit(solution)/shard_map/pallas_call | solution.py:172
  186.8 20.6 %all_to_all.46 = bf16[16,128,256]{2,1,0:T(8,128)(2,1)S(1)} all-to-all(bf16[16,128,256]{2,1,0:T(8,128)(2,1)S(1)} %bitcast.68), channel_id=1, replica_groups=mesh['x'=4,'z'=8,'core'=2,'group'=4] {'x','group'}, dimensions={0} | all-to-all | bytes 2097152 | tf_op jit(solution)/shard_map/all_to_all | solution.py:274
  207.5 11.5 %all_to_all.47 = f32[8,16,256]{2,1,0:T(8,128)S(1)} all-to-all(f32[8,16,256]{2,1,0:T(8,128)S(1)} %convert_add_fusion), channel_id=1, replica_groups=mesh['x'=4,'z'=8,'core'=2,'group'=4] {'z'}, dimensions={0} | all-to-all | bytes 262144 | tf_op jit(solution)/shard_map/all_to_all | solution.py:277
  219.0 0.6 fusion.34
  (54 shorter events, 2.4 us)
Async XLA Ops:
  1.4 18.5 %all-to-all-start = ((s32[8,1,1024]{2,1,0:T(1,128)}), s32[8,1,1024]{2,1,0:T(1,128)S(1)}, u32[]{:S(2)}, u32[]{:S(2)}) async-start(s32[8,1,1024]{2,1,0:T(1,128)} %all_to_all.30), calls=%async_computation | async-start | bytes 65536 | tf_op jit(solution)/shard_map/all_to_all | solution.py:210
  19.9 112.7 %all-to-all-start.1 = ((bf16[256,8,1024]{2,1,0:T(8,128)(2,1)}), bf16[256,8,1024]{2,1,0:T(8,128)(2,1)}, u32[]{:S(2)}, u32[]{:S(2)}) async-start(bf16[256,8,1024]{2,1,0:T(8,128)(2,1)} %bitcast.70), calls=%async_computation.1 | async-start | bytes 8388608 | tf_op jit(solution)/shard_map/all_to_all | solution.py:216
  43.3 5.2 %collective-permute-start = (s32[8,128]{1,0:T(8,128)S(1)}, s32[8,128]{1,0:T(8,128)S(1)}, u32[]{:S(2)}, u32[]{:S(2)}) collective-permute-start(s32[8,128]{1,0:T(8,128)S(1)} %select_bitcast_fusion.12), channel_id=1, source_target_pairs={{0,128},{64,192},{128,0},{192,64},{1,129},{65,193},{129,1},{193,65... | collective-permute-start | bytes 12296 | tf_op jit(solution)/shard_map/ppermute | solution.py:41
  48.6 3.7 %collective-permute-start.1 = (s32[16,64]{1,0:T(8,128)S(1)}, s32[16,64]{1,0:T(8,128)S(1)}, u32[]{:S(2)}, u32[]{:S(2)}) collective-permute-start(s32[16,64]{1,0:T(8,128)S(1)} %select_bitcast_fusion.11), channel_id=1, source_target_pairs={{0,64},{64,0},{128,192},{192,128},{1,65},{65,1},{129,193},{193,129... | collective-permute-start | bytes 12296 | tf_op jit(solution)/shard_map/ppermute | solution.py:41
  52.6 1.3 collective-permute-start.2
  54.1 5.7 %collective-permute-start.3 = (s32[64,16]{1,0:T(8,128)S(1)}, s32[64,16]{1,0:T(8,128)S(1)}, u32[]{:S(2)}, u32[]{:S(2)}) collective-permute-start(s32[64,16]{1,0:T(8,128)S(1)} %select_bitcast_fusion.5), channel_id=1, source_target_pairs={{0,2},{1,3},{2,0},{3,1},{4,6},{5,7},{6,4},{7,5},{8,10},{9,11},{10,... | collective-permute-start | bytes 12296 | tf_op jit(solution)/shard_map/ppermute | solution.py:41
  60.1 6.0 %collective-permute-start.4 = (s32[128,8]{1,0:T(8,128)S(1)}, s32[128,8]{1,0:T(8,128)S(1)}, u32[]{:S(2)}, u32[]{:S(2)}) collective-permute-start(s32[128,8]{1,0:T(8,128)S(1)} %select_bitcast_fusion.2), channel_id=1, source_target_pairs={{0,1},{1,0},{2,3},{3,2},{4,5},{5,4},{6,7},{7,6},{8,9},{9,8},{10,11... | collective-permute-start | bytes 12296 | tf_op jit(solution)/shard_map/ppermute | solution.py:41
  138.6 41.2 %all-to-all-start.2 = ((bf16[256,2,1152]{2,1,0:T(2,128)(2,1)}), bf16[256,2,1152]{2,1,0:T(2,128)(2,1)S(1)}, u32[]{:S(2)}, u32[]{:S(2)}) async-start(bf16[256,2,1152]{2,1,0:T(2,128)(2,1)} %all_to_all.36), calls=%async_computation.2 | async-start | bytes 2359296 | tf_op jit(solution)/shard_map/all_to_all | solution.py:247
  146.2 1.0 copy-start.1
  146.3 2.8 %collective-permute-start.6 = (bf16[512,1024]{1,0:T(8,128)(2,1)S(1)}, bf16[512,1024]{1,0:T(8,128)(2,1)S(1)}, u32[]{:S(2)}, u32[]{:S(2)}) collective-permute-start(bf16[512,1024]{1,0:T(8,128)(2,1)S(1)} %convolution_convert_fusion), channel_id=1, source_target_pairs={{0,4},{4,0},{1,5},{5,1},{2,6},{6,2},{3,7},{7,3},{8,12},{12,8},{9,1... | collective-permute-start | bytes 3145736 | tf_op jit(solution)/shard_map/ppermute | solution.py:41
  146.5 4.1 %collective-permute-start.5 = (bf16[512,1024]{1,0:T(8,128)(2,1)S(1)}, bf16[512,1024]{1,0:T(8,128)(2,1)}, u32[]{:S(2)}, u32[]{:S(2)}) collective-permute-start(bf16[512,1024]{1,0:T(8,128)(2,1)S(1)} %slice.168), channel_id=1, source_target_pairs={{0,4},{4,0},{1,5},{5,1},{2,6},{6,2},{3,7},{7,3},{8,12},{12,8},{9,1... | collective-permute-start | bytes 3145736 | tf_op jit(solution)/shard_map/ppermute | solution.py:41
  149.0 1.0 copy-start.2
  180.6 2.0 collective-permute-start.7
  182.6 1.6 copy-start

commit v7 on v6

--- a/solution.py
+++ b/solution.py
@@ -185,7 +185,7 @@
             pltpu.VMEM((2 * firms, width), jnp.bfloat16),
             pltpu.VMEM((picked, 4 * firms), jnp.bfloat16),
         ],
-        compiler_params=pltpu.CompilerParams(vmem_limit_bytes=12 * 1024 * 1024),
+        compiler_params=pltpu.CompilerParams(vmem_limit_bytes=52 * 1024 * 1024),
         cost_estimate=pl.CostEstimate(
             flops=2 * picked * width * 10 * firms, bytes_accessed=6 * 1024 * 1024, transcendentals=0
         ),

time: 220 us -> 222 us (level)
  Pallas kernels: 15 us -> 17.9 us
  local copies, waits for them, and re-layouts: 6.54 us -> 4.31 us
    pallas_call x1, Pallas kernels: 2.53 us -> 5.4 us  [all_terms(): pl.pallas_call(kernel, grid=(col_parts,), in_specs=[pl.BlockSpec((2 * fir...]
where the time goes in v7:
time: 222 us; the launch traced here: 221 us
  waiting for transfers between devices  104 us (47%)
  starting transfers between devices  39.1 us (18%)
  blocking collectives  32.7 us (15%)
  Pallas kernels  17.9 us (8%)
  other arithmetic  17.1 us (8%)
  matrix products  6.17 us (3%)
  local copies, waits for them, and re-layouts  4.31 us (2%)
    all_to_all x1, waiting for transfers between devices, local(): got = lax.all_to_all(packed, EVERYONE, 0, 0, tiled=True)  63.5 us
    all_to_all x1, waiting for transfers between devices, local(): came = lax.all_to_all(sent, EVERYONE, 0, 0, tiled=True)  23.8 us
    all_to_all x1, blocking collectives, local(): terms = lax.all_to_all(terms, ('x', 'group'), 0, 0, tiled=True)  21.2 us
    ppermute x8, waiting for transfers between devices, swapped(): return lax.ppermute(value, axis, [(i, i ^ bit) for i in range(size)])  16.5 us
    all_to_all x1, starting transfers between devices, local(): got = lax.all_to_all(packed, EVERYONE, 0, 0, tiled=True)  14.3 us
    all_to_all x1, blocking collectives, local(): lax.all_to_all(terms.reshape(z_count, block_rows, block_cols), 'z', 0, 0,...  11.5 us
    ppermute x8, starting transfers between devices, swapped(): return lax.ppermute(value, axis, [(i, i ^ bit) for i in range(size)])  9.82 us
    all_to_all x1, starting transfers between devices, local(): raw = lax.all_to_all(raw, 'z', 0, 0, tiled=True)  8.47 us
  transfers between devices with their start and end apart: 11, of which 10 were waited for; matrix products, arithmetic and copies ran while one was open for 10% of the time, Pallas kernels for 3%

profile of v7, /device:TPU:8, one launch (start us, length us, event | category | flops | bytes accessed | tf_op | source)
XLA Modules:
  0.0 221.4 jit_solution(11065910500757422244)
XLA Ops:
  0.0 0.7 multiply_add_fusion.1
  0.7 0.6 all_to_all.30
  1.3 8.5 %all-to-all-start = ((s32[8,1,1024]{2,1,0:T(1,128)}), s32[8,1,1024]{2,1,0:T(1,128)S(1)}, u32[]{:S(2)}, u32[]{:S(2)}) async-start(s32[8,1,1024]{2,1,0:T(1,128)} %all_to_all.30), calls=%async_computation | async-start | bytes 65536 | tf_op jit(solution)/shard_map/all_to_all | solution.py:210
  9.8 0.7 add_select_fusion.12
  10.5 0.4 convert_reduce_fusion.1
  10.9 1.3 multiply_add_fusion
  12.2 7.6 %shard_map.37 = bf16[2048,1024]{1,0:T(8,128)(2,1)} custom-call(s32[1,1024]{1,0:T(1,128)} %bitcast.92, bf16[1024,1024]{1,0:T(8,128)(2,1)} %rows_ref.1), custom_call_target="tpu_custom_call" | custom-call | flops 4294967296 | bytes 6291456 | tf_op jit(solution)/shard_map/pallas_call | solution.py:72
  19.9 14.3 %all-to-all-start.1 = ((bf16[256,8,1024]{2,1,0:T(8,128)(2,1)}), bf16[256,8,1024]{2,1,0:T(8,128)(2,1)}, u32[]{:S(2)}, u32[]{:S(2)}) async-start(bf16[256,8,1024]{2,1,0:T(8,128)(2,1)} %bitcast.70), calls=%async_computation.1 | async-start | bytes 8388608 | tf_op jit(solution)/shard_map/all_to_all | solution.py:216
  34.2 0.3 iota_compare_fusion.1
  34.6 7.2 %convert_reduce_fusion = s32[8,1024]{1,0:T(8,128)S(1)} fusion(s32[8,1024]{1,0:T(8,128)S(1)} %fusion.22, pred[1024,1024]{1,0:T(8,128)(4,1)S(1)} %iota_compare_fusion.1), kind=kLoop, calls=%fused_computation | loop fusion | flops 33546240 | bytes 1114112 | tf_op jit(solution)/shard_map/vmap()/reduce_sum | solution.py:18
  42.0 1.2 select_reduce_fusion
  43.2 3.1 %collective-permute-start = (s32[8,128]{1,0:T(8,128)S(1)}, s32[8,128]{1,0:T(8,128)S(1)}, u32[]{:S(2)}, u32[]{:S(2)}) collective-permute-start(s32[8,128]{1,0:T(8,128)S(1)} %select_bitcast_fusion.12), channel_id=1, source_target_pairs={{0,128},{64,192},{128,0},{192,64},{1,129},{65,193},{129,1},{193,65... | collective-permute-start | bytes 12296 | tf_op jit(solution)/shard_map/ppermute | solution.py:41
  46.3 2.2 collective-permute-done
  48.6 1.5 collective-permute-start.1
  50.1 2.2 %collective-permute-done.1 = s32[16,64]{1,0:T(8,128)S(1)} collective-permute-done((s32[16,64]{1,0:T(8,128)S(1)}, s32[16,64]{1,0:T(8,128)S(1)}, u32[]{:S(2)}, u32[]{:S(2)}) %collective-permute-start.1) | collective-permute-done | bytes 4128 | tf_op jit(solution)/shard_map/ppermute | solution.py:41
  52.6 1.2 collective-permute-done.2
  54.0 2.2 collective-permute-start.3
  56.2 3.5 %collective-permute-done.3 = s32[64,16]{1,0:T(8,128)S(1)} collective-permute-done((s32[64,16]{1,0:T(8,128)S(1)}, s32[64,16]{1,0:T(8,128)S(1)}, u32[]{:S(2)}, u32[]{:S(2)}) %collective-permute-start.3) | collective-permute-done | bytes 4128 | tf_op jit(solution)/shard_map/ppermute | solution.py:41
  60.1 2.5 %collective-permute-start.4 = (s32[128,8]{1,0:T(8,128)S(1)}, s32[128,8]{1,0:T(8,128)S(1)}, u32[]{:S(2)}, u32[]{:S(2)}) collective-permute-start(s32[128,8]{1,0:T(8,128)S(1)} %select_bitcast_fusion.2), channel_id=1, source_target_pairs={{0,1},{1,0},{2,3},{3,2},{4,5},{5,4},{6,7},{7,6},{8,9},{9,8},{10,11... | collective-permute-start | bytes 12296 | tf_op jit(solution)/shard_map/ppermute | solution.py:41
  62.6 3.5 %collective-permute-done.4 = s32[128,8]{1,0:T(8,128)S(1)} collective-permute-done((s32[128,8]{1,0:T(8,128)S(1)}, s32[128,8]{1,0:T(8,128)S(1)}, u32[]{:S(2)}, u32[]{:S(2)}) %collective-permute-start.4) | collective-permute-done | bytes 4128 | tf_op jit(solution)/shard_map/ppermute | solution.py:41
  66.3 0.2 reshape_reshape.3
  66.6 0.4 select_reduce_fusion.4
  66.9 0.4 select_reduce_fusion.3
  67.3 0.6 select_reduce_fusion.2
  68.0 0.2 convert_reduce_fusion.2
  68.2 0.2 select_reduce_fusion.6
  68.4 0.7 select_reduce_fusion.1
  69.1 63.5 %all-to-all-done.1 = bf16[256,8,1024]{2,1,0:T(8,128)(2,1)} async-done(((bf16[256,8,1024]{2,1,0:T(8,128)(2,1)}), bf16[256,8,1024]{2,1,0:T(8,128)(2,1)}, u32[]{:S(2)}, u32[]{:S(2)}) %all-to-all-start.1) | async-done | bytes 4194336 | tf_op jit(solution)/shard_map/all_to_all | solution.py:216
  132.7 4.5 %shard_map.38 = bf16[512,1152]{1,0:T(8,128)(2,1)S(1)} custom-call(s32[1,2048]{1,0:T(1,128)S(1)} %bitcast.68, bf16[2048,1024]{1,0:T(8,128)(2,1)} %bitcast.33.rows_ref, bf16[512,128]{1,0:T(8,128)(2,1)S(1)} %broadcast_in_dim.152.tail_ref), custom_call_target="tpu_custom_call" | custom-call | flops 2147483648 | bytes 6291456 | tf_op jit(solution)/shard_map/pallas_call | solution.py:107
  137.2 1.3 all_to_all.36
  138.5 6.5 %all-to-all-start.2 = ((bf16[256,2,1152]{2,1,0:T(2,128)(2,1)}), bf16[256,2,1152]{2,1,0:T(2,128)(2,1)S(1)}, u32[]{:S(2)}, u32[]{:S(2)}) async-start(bf16[256,2,1152]{2,1,0:T(2,128)(2,1)} %all_to_all.36), calls=%async_computation.2 | async-start | bytes 2359296 | tf_op jit(solution)/shard_map/all_to_all | solution.py:247
  145.1 0.2 select_reduce_fusion.5
  145.4 0.8 convolution_convert_fusion
  146.2 0.2 collective-permute-start.6
  146.4 0.7 copy-done
  147.2 0.1 collective-permute-start.5
  147.3 1.2 fusion.8.pick_ref
  148.6 0.4 collective-permute-done.6
  149.0 1.6 collective-permute-done.5
  150.6 5.4 %fusion.4.terms_ref = f32[512,1024]{1,0:T(8,128)} fusion(bf16[512,1024]{1,0:T(8,128)(2,1)S(1)} %collective-permute-done.6, bf16[512,1024]{1,0:T(8,128)(2,1)} %copy-done, bf16[512,1024]{1,0:T(8,128)(2,1)} %collective-permute-done.5, bf16[512,1024]{1,0:T(8,128)(2,1)S(1)} %slice.168, s32[512]{0:T(512)S(1)} %fusion.48), kind=kOutput, calls=%fused_computation.12 | convolution fusion | flops 2156920832 | bytes 6293504 | tf_op jit(solution)/shard_map/dot_general | solution.py:36
  156.0 23.8 %all-to-all-done.2 = bf16[256,2,1152]{2,1,0:T(2,128)(2,1)S(1)} async-done(((bf16[256,2,1152]{2,1,0:T(2,128)(2,1)}), bf16[256,2,1152]{2,1,0:T(2,128)(2,1)S(1)}, u32[]{:S(2)}, u32[]{:S(2)}) %all-to-all-start.2) | async-done | bytes 1179680 | tf_op jit(solution)/shard_map/all_to_all | solution.py:247
  179.8 0.5 all_to_all.38.came_ref
  180.3 0.3 shard_map.39.own_ref
  180.7 1.9 collective-permute-done.7.other_ref
  182.6 5.4 %shard_map.40 = bf16[4,4,128,256]{3,2,1,0:T(8,128)(2,1)} custom-call(bf16[256,1024]{1,0:T(8,128)(2,1)S(1)} %shard_map.39.own_ref, bf16[256,1024]{1,0:T(8,128)(2,1)S(1)} %collective-permute-done.7.other_ref, bf16[512,1024]{1,0:T(8,128)(2,1)} %fusion.8.pick_ref, f32[512,1024]{1,0:T(8,128)} %fusion.4.terms_ref), custom_call_target="tpu_custom_call" | custom-call | flops 1342177280 | bytes 6291456 | tf_op jit(solution)/shard_map/pallas_call | solution.py:172
  188.0 21.2 %all_to_all.46 = bf16[16,128,256]{2,1,0:T(8,128)(2,1)S(1)} all-to-all(bf16[16,128,256]{2,1,0:T(8,128)(2,1)} %bitcast.69), channel_id=1, replica_groups=mesh['x'=4,'z'=8,'core'=2,'group'=4] {'x','group'}, dimensions={0} | all-to-all | bytes 2097152 | tf_op jit(solution)/shard_map/all_to_all | solution.py:274
  209.4 11.5 %all_to_all.47 = f32[8,16,256]{2,1,0:T(8,128)S(1)} all-to-all(f32[8,16,256]{2,1,0:T(8,128)S(1)} %convert_add_fusion), channel_id=1, replica_groups=mesh['x'=4,'z'=8,'core'=2,'group'=4] {'z'}, dimensions={0} | all-to-all | bytes 262144 | tf_op jit(solution)/shard_map/all_to_all | solution.py:277
  220.8 0.6 fusion.34
  (50 shorter events, 2.0 us)
Async XLA Ops:
  1.3 18.5 %all-to-all-start = ((s32[8,1,1024]{2,1,0:T(1,128)}), s32[8,1,1024]{2,1,0:T(1,128)S(1)}, u32[]{:S(2)}, u32[]{:S(2)}) async-start(s32[8,1,1024]{2,1,0:T(1,128)} %all_to_all.30), calls=%async_computation | async-start | bytes 65536 | tf_op jit(solution)/shard_map/all_to_all | solution.py:210
  19.9 112.7 %all-to-all-start.1 = ((bf16[256,8,1024]{2,1,0:T(8,128)(2,1)}), bf16[256,8,1024]{2,1,0:T(8,128)(2,1)}, u32[]{:S(2)}, u32[]{:S(2)}) async-start(bf16[256,8,1024]{2,1,0:T(8,128)(2,1)} %bitcast.70), calls=%async_computation.1 | async-start | bytes 8388608 | tf_op jit(solution)/shard_map/all_to_all | solution.py:216
  43.2 5.2 %collective-permute-start = (s32[8,128]{1,0:T(8,128)S(1)}, s32[8,128]{1,0:T(8,128)S(1)}, u32[]{:S(2)}, u32[]{:S(2)}) collective-permute-start(s32[8,128]{1,0:T(8,128)S(1)} %select_bitcast_fusion.12), channel_id=1, source_target_pairs={{0,128},{64,192},{128,0},{192,64},{1,129},{65,193},{129,1},{193,65... | collective-permute-start | bytes 12296 | tf_op jit(solution)/shard_map/ppermute | solution.py:41
  48.6 3.7 %collective-permute-start.1 = (s32[16,64]{1,0:T(8,128)S(1)}, s32[16,64]{1,0:T(8,128)S(1)}, u32[]{:S(2)}, u32[]{:S(2)}) collective-permute-start(s32[16,64]{1,0:T(8,128)S(1)} %select_bitcast_fusion.11), channel_id=1, source_target_pairs={{0,64},{64,0},{128,192},{192,128},{1,65},{65,1},{129,193},{193,129... | collective-permute-start | bytes 12296 | tf_op jit(solution)/shard_map/ppermute | solution.py:41
  52.5 1.3 collective-permute-start.2
  54.0 5.7 %collective-permute-start.3 = (s32[64,16]{1,0:T(8,128)S(1)}, s32[64,16]{1,0:T(8,128)S(1)}, u32[]{:S(2)}, u32[]{:S(2)}) collective-permute-start(s32[64,16]{1,0:T(8,128)S(1)} %select_bitcast_fusion.5), channel_id=1, source_target_pairs={{0,2},{1,3},{2,0},{3,1},{4,6},{5,7},{6,4},{7,5},{8,10},{9,11},{10,... | collective-permute-start | bytes 12296 | tf_op jit(solution)/shard_map/ppermute | solution.py:41
  60.1 6.0 %collective-permute-start.4 = (s32[128,8]{1,0:T(8,128)S(1)}, s32[128,8]{1,0:T(8,128)S(1)}, u32[]{:S(2)}, u32[]{:S(2)}) collective-permute-start(s32[128,8]{1,0:T(8,128)S(1)} %select_bitcast_fusion.2), channel_id=1, source_target_pairs={{0,1},{1,0},{2,3},{3,2},{4,5},{5,4},{6,7},{7,6},{8,9},{9,8},{10,11... | collective-permute-start | bytes 12296 | tf_op jit(solution)/shard_map/ppermute | solution.py:41
  138.5 41.2 %all-to-all-start.2 = ((bf16[256,2,1152]{2,1,0:T(2,128)(2,1)}), bf16[256,2,1152]{2,1,0:T(2,128)(2,1)S(1)}, u32[]{:S(2)}, u32[]{:S(2)}) async-start(bf16[256,2,1152]{2,1,0:T(2,128)(2,1)} %all_to_all.36), calls=%async_computation.2 | async-start | bytes 2359296 | tf_op jit(solution)/shard_map/all_to_all | solution.py:247
  146.2 1.0 copy-start
  146.2 2.7 %collective-permute-start.6 = (bf16[512,1024]{1,0:T(8,128)(2,1)S(1)}, bf16[512,1024]{1,0:T(8,128)(2,1)S(1)}, u32[]{:S(2)}, u32[]{:S(2)}) collective-permute-start(bf16[512,1024]{1,0:T(8,128)(2,1)S(1)} %convolution_convert_fusion), channel_id=1, source_target_pairs={{0,4},{4,0},{1,5},{5,1},{2,6},{6,2},{3,7},{7,3},{8,12},{12,8},{9,1... | collective-permute-start | bytes 3145736 | tf_op jit(solution)/shard_map/ppermute | solution.py:41
  147.2 3.4 %collective-permute-start.5 = (bf16[512,1024]{1,0:T(8,128)(2,1)S(1)}, bf16[512,1024]{1,0:T(8,128)(2,1)}, u32[]{:S(2)}, u32[]{:S(2)}) collective-permute-start(bf16[512,1024]{1,0:T(8,128)(2,1)S(1)} %slice.168), channel_id=1, source_target_pairs={{0,4},{4,0},{1,5},{5,1},{2,6},{6,2},{3,7},{7,3},{8,12},{12,8},{9,1... | collective-permute-start | bytes 3145736 | tf_op jit(solution)/shard_map/ppermute | solution.py:41
  180.6 2.0 collective-permute-start.7
